TPU v7x, 32 devices: a whole 2x2x4 slice. The times are simulated.
32 devices in a mesh: batch: 8 (over z, core), seq: 4 (over y, x).
Axes of the slice: x: 2, y: 2, z: 4, core: 2. Of those that a mesh axis runs over, the one named last changes fastest.
Arguments:
- image_in: bfloat16 [1024, 8, 1152], P('seq', 'batch'), may hold values from -6 to 6
- cond_in: bfloat16 [78, 8, 1152], P(None, 'batch'), may hold values from -6 to 6
- skip_image: bfloat16 [1024, 8, 1152], P('seq', 'batch'), may hold values from -6 to 6
- skip_cond: bfloat16 [78, 8, 1152], P(None, 'batch'), may hold values from -6 to 6
- caption_len: int32 [8], P('batch'), may hold values from 1 to 77, as said below
- skip_weight: bfloat16 [2304, 1152], replicated, may hold values from -0.125 to 0.125
- skip_bias: float32 [1152], replicated, may hold values from -4 to 4
- first_gain: float32 [1152], replicated, may hold values from 0.5 to 1.5
- first_bias: float32 [1152], replicated, may hold values from -4 to 4
- qkv_weight: bfloat16 [1152, 3456], replicated, may hold values from -0.1875 to 0.1875
- proj_weight: bfloat16 [1152, 1152], replicated, may hold values from -3 to 3
- proj_bias: float32 [1152], replicated, may hold values from -4 to 4
- second_gain: float32 [1152], replicated, may hold values from 0.5 to 1.5
- second_bias: float32 [1152], replicated, may hold values from -4 to 4
- fc1_weight: bfloat16 [1152, 4608], replicated, may hold values from -0.1875 to 0.1875
- fc1_bias: float32 [4608], replicated, may hold values from -4 to 4
- fc2_weight: bfloat16 [4608, 1152], replicated, may hold values from -0.09375 to 0.09375
- fc2_bias: float32 [1152], replicated, may hold values from -4 to 4
- grad_image: bfloat16 [1024, 8, 1152], P('seq', 'batch'), may hold values from -6 to 6
- grad_cond: bfloat16 [78, 8, 1152], P(None, 'batch'), may hold values from -6 to 6
Outputs:
- out_image: float32 [1024, 8, 1152], P('seq', 'batch')
- out_cond: float32 [78, 8, 1152], P(None, 'batch')
- dgrad_image_in: float32 [1024, 8, 1152], P('seq', 'batch')
- dgrad_cond_in: float32 [78, 8, 1152], P(None, 'batch')
- dgrad_skip_image: float32 [1024, 8, 1152], P('seq', 'batch')
- dgrad_skip_cond: float32 [78, 8, 1152], P(None, 'batch')
- wgrad_skip_weight: float32 [2304, 1152], P('batch')
- wgrad_skip_bias: float32 [1152], P('batch')
- wgrad_first_gain: float32 [1152], P('batch')
- wgrad_first_bias: float32 [1152], P('batch')
- wgrad_qkv_weight: float32 [1152, 3456], P('batch')
- wgrad_proj_weight: float32 [1152, 1152], P('batch')
- wgrad_proj_bias: float32 [1152], P('batch')
- wgrad_second_gain: float32 [1152], P('batch')
- wgrad_second_bias: float32 [1152], P('batch')
- wgrad_fc1_weight: float32 [1152, 4608], P('batch')
- wgrad_fc1_bias: float32 [4608], P('batch')
- wgrad_fc2_weight: float32 [4608, 1152], P('batch')
- wgrad_fc2_bias: float32 [1152], P('batch')
Inputs may be any that keep to these rules, and one draw needn't show every extreme that they name: `caption_len`: every item has at least one valid caption token; some item has all 77 valid and some item exactly one.
All inputs are finite; a program needn't handle non-finite values.
Results may differ from a plain program's by a relative error of at most 0.02.
Values may be sent and summed in bfloat16 or wider, within the bound.
A program may use at most 256 MiB of HBM per device.

v0:
```python
import math

import jax
import jax.numpy as jnp
from jax import lax
from jax.sharding import PartitionSpec as P

HEADS = 16
HEAD_DIM = 72


def shortened(value):

    def short(part):
        return part.astype(jnp.bfloat16) if part.dtype == jnp.float32 else part

    return jax.tree.map(short, value)


def contract_rows(left, right):
    return lax.dot_general(
        left, right, (((0,), (0,)), ((), ())), preferred_element_type=jnp.float32
    )


def times_transpose(left, right):
    return lax.dot_general(
        left, right, (((1,), (1,)), ((), ())), preferred_element_type=jnp.float32
    )


def normalize(values):
    centre = values - jnp.mean(values, axis=-1, keepdims=True)
    factor = lax.rsqrt(jnp.mean(centre * centre, axis=-1, keepdims=True) + 1e-05)
    return (centre * factor, factor)


def norm_back(upstream, scaled, factor, norm_gain):
    inner_term = upstream * norm_gain
    centred = inner_term - jnp.mean(inner_term, axis=-1, keepdims=True)
    return factor * (centred - scaled * jnp.mean(inner_term * scaled, axis=-1, keepdims=True))


def gelu_exact(values):
    return jax.nn.gelu(values, approximate=False)


def per_device(
    image_in,
    cond_in,
    skip_image,
    skip_cond,
    caption_len,
    skip_weight,
    skip_bias,
    first_gain,
    first_bias,
    qkv_weight,
    proj_weight,
    proj_bias,
    second_gain,
    second_bias,
    fc1_weight,
    fc1_bias,
    fc2_weight,
    fc2_bias,
    grad_image,
    grad_cond,
):
    cond_rows = cond_in.shape[0]
    image_rows = image_in.shape[0]
    batch_items = image_in.shape[1]
    model_width = image_in.shape[2]
    score_scale = 1.0 / math.sqrt(HEAD_DIM)
    lead_in, lead_skip, lead_cot = (cond_in, skip_cond, grad_cond)
    own_flag = (lax.axis_index("seq") == 0).astype(jnp.float32)
    row_count = cond_rows + image_rows
    flat_rows = row_count * batch_items
    inputs = jnp.concatenate([lead_in, image_in], 0)
    skips = jnp.concatenate([lead_skip, skip_image], 0)
    joined = jnp.concatenate([inputs, skips], -1).reshape(flat_rows, 2 * model_width)
    hidden = jnp.dot(joined, skip_weight, preferred_element_type=jnp.float32) + skip_bias
    first_scaled, first_factor = normalize(hidden)
    normed = (first_scaled * first_gain + first_bias).astype(jnp.bfloat16)
    triple = jnp.dot(normed, qkv_weight, preferred_element_type=jnp.float32).astype(jnp.bfloat16)
    triple = triple.reshape(row_count, batch_items, 3 * model_width)
    queries = triple[:, :, :model_width].reshape(row_count, batch_items, HEADS, HEAD_DIM)
    local_pairs = triple[:, :, model_width:]
    gathered = lax.all_gather(local_pairs[cond_rows:], "seq", axis=0, tiled=True)
    key_values = jnp.concatenate([local_pairs[:cond_rows], gathered], 0)
    span_keys = key_values.shape[0]
    positions = lax.broadcasted_iota(jnp.int32, (batch_items, span_keys), 1)
    allowed = (positions <= caption_len[:, None]) | (positions >= cond_rows)
    key_mask = allowed[:, None, None, :]

    def split_heads(pairs):
        key_heads = pairs[:, :, :model_width].reshape(span_keys, batch_items, HEADS, HEAD_DIM)
        value_heads = pairs[:, :, model_width:].reshape(span_keys, batch_items, HEADS, HEAD_DIM)
        return (key_heads, value_heads)

    def attend_scores(key_heads):
        raw_scores = jnp.einsum(
            "qbhd,kbhd->bhqk", queries, key_heads, preferred_element_type=jnp.float32
        )
        return jnp.where(key_mask, raw_scores * score_scale, -1e30)

    key_heads, value_heads = split_heads(key_values)
    scores = attend_scores(key_heads)
    row_peak = jnp.max(scores, axis=-1, keepdims=True)
    shifted = jnp.exp(scores - row_peak)
    row_sum = jnp.sum(shifted, axis=-1, keepdims=True)
    attn_probs = (shifted / row_sum).astype(jnp.bfloat16)
    log_total = row_peak + jnp.log(row_sum)
    context = jnp.einsum(
        "bhqk,kbhd->qbhd", attn_probs, value_heads, preferred_element_type=jnp.float32
    )
    context = context.astype(jnp.bfloat16).reshape(flat_rows, model_width)
    middle = hidden + jnp.dot(context, proj_weight, preferred_element_type=jnp.float32) + proj_bias
    second_scaled, second_factor = normalize(middle)
    normed_two = (second_scaled * second_gain + second_bias).astype(jnp.bfloat16)
    pre_gelu = jnp.dot(normed_two, fc1_weight, preferred_element_type=jnp.float32) + fc1_bias
    active = gelu_exact(pre_gelu).astype(jnp.bfloat16)
    output = middle + jnp.dot(active, fc2_weight, preferred_element_type=jnp.float32) + fc2_bias
    output = output.reshape(row_count, batch_items, model_width)
    row_weight = jnp.concatenate(
        [own_flag * jnp.ones((cond_rows,), jnp.float32), jnp.ones((image_rows,), jnp.float32)]
    )
    row_flat = row_weight[:, None]
    weight_low = row_flat.astype(jnp.bfloat16)
    query_weight = row_weight.astype(jnp.bfloat16)[None, None, :, None]
    cotangent = jnp.concatenate([lead_cot, grad_image], 0).reshape(flat_rows, model_width)
    weighted_cot = cotangent * weight_low
    wgrad_fc2_weight = contract_rows(active, weighted_cot)
    wgrad_fc2_bias = jnp.sum(weighted_cot.astype(jnp.float32), 0)
    d_active = times_transpose(cotangent, fc2_weight)
    d_pre = jax.vjp(gelu_exact, pre_gelu)[1](d_active)[0].astype(jnp.bfloat16)
    weighted_pre = d_pre * weight_low
    wgrad_fc1_weight = contract_rows(normed_two, weighted_pre)
    wgrad_fc1_bias = jnp.sum(weighted_pre.astype(jnp.float32), 0)
    d_second = times_transpose(d_pre, fc1_weight)
    wgrad_second_gain = jnp.sum(d_second * second_scaled * row_flat, 0)
    wgrad_second_bias = jnp.sum(d_second * row_flat, 0)
    mlp_grads = (
        wgrad_second_gain,
        wgrad_second_bias,
        wgrad_fc1_weight,
        wgrad_fc1_bias,
        wgrad_fc2_weight,
        wgrad_fc2_bias,
    )
    d_middle = cotangent.astype(jnp.float32) + norm_back(
        d_second, second_scaled, second_factor, second_gain
    )
    d_branch = d_middle.astype(jnp.bfloat16)
    weighted_branch = d_branch * weight_low
    wgrad_proj_weight = contract_rows(context, weighted_branch)
    wgrad_proj_bias = jnp.sum(weighted_branch.astype(jnp.float32), 0)
    d_context = times_transpose(d_branch, proj_weight).astype(jnp.bfloat16)
    d_context = d_context.reshape(row_count, batch_items, HEADS, HEAD_DIM)
    regathered = lax.all_gather(local_pairs[cond_rows:], "seq", axis=0, tiled=True)
    back_pairs = jnp.concatenate([local_pairs[:cond_rows], regathered], 0)
    back_keys, back_values = split_heads(back_pairs)
    fresh_probs = jnp.exp(attend_scores(back_keys) - log_total)
    d_probs = jnp.einsum(
        "qbhd,kbhd->bhqk", d_context, back_values, preferred_element_type=jnp.float32
    )
    row_delta = jnp.sum(fresh_probs * d_probs, axis=-1, keepdims=True)
    d_raw = (fresh_probs * (d_probs - row_delta) * score_scale).astype(jnp.bfloat16)
    d_queries = jnp.einsum("bhqk,kbhd->qbhd", d_raw, back_keys, preferred_element_type=jnp.float32)
    d_queries = d_queries.astype(jnp.bfloat16).reshape(row_count, batch_items, model_width)
    raw_weighted = d_raw * query_weight
    probs_weighted = fresh_probs.astype(jnp.bfloat16) * query_weight
    cond_keys = jnp.einsum(
        "bhqk,qbhd->kbhd",
        raw_weighted[..., :cond_rows],
        queries,
        preferred_element_type=jnp.float32,
    )
    cond_vals = jnp.einsum(
        "bhqk,qbhd->kbhd",
        probs_weighted[..., :cond_rows],
        d_context,
        preferred_element_type=jnp.float32,
    )
    cond_keys, cond_vals = (
        lax.psum(cond_keys.astype(jnp.bfloat16), "seq").astype(jnp.float32),
        lax.psum(cond_vals.astype(jnp.bfloat16), "seq").astype(jnp.float32),
    )
    num_rows = lax.axis_size("seq") * image_rows
    raw_part = lax.dynamic_slice_in_dim(raw_weighted, cond_rows, num_rows, 3)
    prob_part = lax.dynamic_slice_in_dim(probs_weighted, cond_rows, num_rows, 3)
    key_part = jnp.einsum("bhqk,qbhd->kbhd", raw_part, queries, preferred_element_type=jnp.float32)
    value_part = jnp.einsum(
        "bhqk,qbhd->kbhd", prob_part, d_context, preferred_element_type=jnp.float32
    )
    image_pairs = lax.psum_scatter(
        jnp.concatenate(
            [
                key_part.reshape(num_rows, batch_items, model_width),
                value_part.reshape(num_rows, batch_items, model_width),
            ],
            -1,
        ).astype(jnp.bfloat16),
        "seq",
        scatter_dimension=0,
        tiled=True,
    ).astype(jnp.float32)
    d_keys = jnp.concatenate(
        [cond_keys.reshape(cond_rows, batch_items, model_width), image_pairs[:, :, :model_width]], 0
    )
    d_values = jnp.concatenate(
        [cond_vals.reshape(cond_rows, batch_items, model_width), image_pairs[:, :, model_width:]], 0
    )
    d_triple = jnp.concatenate(
        [d_queries, d_keys.astype(jnp.bfloat16), d_values.astype(jnp.bfloat16)], -1
    )
    d_triple = d_triple.reshape(flat_rows, 3 * model_width)
    wgrad_qkv_weight = contract_rows(normed, d_triple * weight_low)
    d_first = times_transpose(d_triple, qkv_weight)
    wgrad_first_gain = jnp.sum(d_first * first_scaled * row_flat, 0)
    wgrad_first_bias = jnp.sum(d_first * row_flat, 0)
    d_hidden = d_middle + norm_back(d_first, first_scaled, first_factor, first_gain)
    d_hidden_low = d_hidden.astype(jnp.bfloat16)
    weighted_hidden = d_hidden_low * weight_low
    wgrad_skip_weight = contract_rows(joined, weighted_hidden)
    wgrad_skip_bias = jnp.sum(weighted_hidden.astype(jnp.float32), 0)
    d_joined = times_transpose(d_hidden_low, skip_weight).reshape(
        row_count, batch_items, 2 * model_width
    )
    rest_grads = (
        wgrad_skip_weight,
        wgrad_skip_bias,
        wgrad_first_gain,
        wgrad_first_bias,
        wgrad_qkv_weight,
        wgrad_proj_weight,
        wgrad_proj_bias,
    )
    every_part = jax.tree.map(
        lambda part: part.astype(jnp.float32),
        lax.psum_scatter(
            shortened(rest_grads + mlp_grads), "batch", scatter_dimension=0, tiled=True
        ),
    )
    column_parts = (
        lax.psum_scatter(
            every_part[0].astype(jnp.bfloat16), "seq", scatter_dimension=1, tiled=True
        ).astype(jnp.float32),
        lax.psum_scatter(
            every_part[4].astype(jnp.bfloat16), "seq", scatter_dimension=1, tiled=True
        ).astype(jnp.float32),
        lax.psum_scatter(
            every_part[5].astype(jnp.bfloat16), "seq", scatter_dimension=1, tiled=True
        ).astype(jnp.float32),
        lax.psum_scatter(
            every_part[9].astype(jnp.bfloat16), "seq", scatter_dimension=1, tiled=True
        ).astype(jnp.float32),
        lax.psum_scatter(
            every_part[11].astype(jnp.bfloat16), "seq", scatter_dimension=1, tiled=True
        ).astype(jnp.float32),
    )
    vector_done = lax.psum(
        (
            every_part[1],
            every_part[2],
            every_part[3],
            every_part[6],
            every_part[7],
            every_part[8],
            every_part[10],
            every_part[12],
        ),
        "seq",
    )
    matrix_done = (
        lax.all_gather(column_parts[0].astype(jnp.bfloat16), "seq", axis=1, tiled=True).astype(
            jnp.float32
        ),
        lax.all_gather(column_parts[1].astype(jnp.bfloat16), "seq", axis=1, tiled=True).astype(
            jnp.float32
        ),
        lax.all_gather(column_parts[2].astype(jnp.bfloat16), "seq", axis=1, tiled=True).astype(
            jnp.float32
        ),
        lax.all_gather(column_parts[3].astype(jnp.bfloat16), "seq", axis=1, tiled=True).astype(
            jnp.float32
        ),
        lax.all_gather(column_parts[4].astype(jnp.bfloat16), "seq", axis=1, tiled=True).astype(
            jnp.float32
        ),
    )
    finished = (
        matrix_done[0],
        vector_done[0],
        vector_done[1],
        vector_done[2],
        matrix_done[1],
        matrix_done[2],
        vector_done[3],
        vector_done[4],
        vector_done[5],
        matrix_done[3],
        vector_done[6],
        matrix_done[4],
        vector_done[7],
    )
    lead_out, lead_din, lead_dskip = (
        output[:cond_rows],
        d_joined[:cond_rows, :, :model_width],
        d_joined[:cond_rows, :, model_width:],
    )
    return (
        output[cond_rows:],
        lead_out,
        d_joined[cond_rows:, :, :model_width],
        lead_din,
        d_joined[cond_rows:, :, model_width:],
        lead_dskip,
        finished[0],
        finished[1],
        finished[2],
        finished[3],
        finished[4],
        finished[5],
        finished[6],
        finished[7],
        finished[8],
        finished[9],
        finished[10],
        finished[11],
        finished[12],
    )


def solution(mesh):
    return jax.shard_map(
        per_device,
        mesh=mesh,
        in_specs=(
            P("seq", "batch", None),
            P(None, "batch", None),
            P("seq", "batch", None),
            P(None, "batch", None),
            P("batch"),
            P(),
            P(),
            P(),
            P(),
            P(),
            P(),
            P(),
            P(),
            P(),
            P(),
            P(),
            P(),
            P(),
            P("seq", "batch", None),
            P(None, "batch", None),
        ),
        out_specs=(
            P("seq", "batch", None),
            P(None, "batch", None),
            P("seq", "batch", None),
            P(None, "batch", None),
            P("seq", "batch", None),
            P(None, "batch", None),
            P("batch", None),
            P("batch"),
            P("batch"),
            P("batch"),
            P("batch", None),
            P("batch", None),
            P("batch"),
            P("batch"),
            P("batch"),
            P("batch", None),
            P("batch"),
            P("batch", None),
            P("batch"),
        ),
        check_vma=False,
    )
```

profile of v0, /device:TPU:0, one launch (start us, length us, event | category | flops | bytes accessed | tf_op | source)
XLA Modules:
  0.0 1035.1 jit_solution(12999675775570669452)
XLA Ops:
  7.3 5.4 fusion.52
  13.1 3.8 fusion.18
  26.8 52.8 %all-gather.6.cloned.1.call-done = bf16[1024,1,2304]{2,0,1:T(8,128)(2,1)} async-done(((bf16[256,1,2304]{2,0,1:T(8,128)(2,1)}), bf16[1024,1,2304]{2,0,1:T(8,128)(2,1)}) %all-gather.6.cloned.1.call-update) | async-done | bytes 4718608 | tf_op jit(solution)/shard_map/all_gather | solution.py:89
  79.6 4.8 pad_maximum_fusion.1
  84.4 5.2 copy.73
  89.6 5.2 copy.71
  94.8 14.3 %fusion.53 = (f32[16,334]{1,0:T(8,128)S(1)}, f32[16,334,1102]{2,1,0:T(8,128)}) fusion(bf16[334,16,72]{0,2,1:T(8,128)(2,1)S(1)} %bitcast.150, bf16[1102,16,72]{0,2,1:T(8,128)(2,1)} %bitcast.148, pred[1102]{0:T(1024)(128)(4,1)S(1)} %fusion.41), kind=kOutput, calls=%fused_computation.133 | convolution fusion | flops 865690624 | bytes 26887374 | tf_op jit(solution)/shard_map/qbhd,kbhd->bhqk/dot_general | solution.py:102
  109.1 11.5 %fusion.4 = f32[16,334]{1,0:T(8,128)S(1)} fusion(f32[16,334,1102]{2,1,0:T(8,128)} %get-tuple-element.121, f32[16,334]{1,0:T(8,128)S(1)} %get-tuple-element.120), kind=kLoop, calls=%fused_computation.8 | loop fusion | flops 11772832 | bytes 23599104 | tf_op jit(solution)/shard_map/reduce_sum | solution.py:111
  121.2 10.5 %fusion.27 = bf16[16,72,334]{2,1,0:T(8,128)(2,1)S(1)} fusion(bf16[1102,16,72]{0,2,1:T(8,128)(2,1)S(1)} %bitcast.163, f32[16,334,1102]{2,1,0:T(8,128)} %get-tuple-element.121, f32[16,334]{1,0:T(8,128)S(1)} %fusion.4, f32[16,334]{1,0:T(8,128)S(1)} %get-tuple-element.120), kind=kOutput, calls=%fused_computation.79 | convolution fusion | flops 866080704 | bytes 26907648 | tf_op jit(solution)/shard_map/bhqk,kbhd->qbhd/dot_general | solution.py:114
  133.7 22.2 %multiply_convert_fusion.1 = (bf16[334,4608]{1,0:T(8,128)(2,1)}, f32[334,4608]{1,0:T(8,128)}, f32[334,4608]{1,0:T(8,128)}) fusion(f32[4608]{0:T(1024)S(1)} %copy-done.47, bf16[1152,4608]{1,0:T(8,128)(2,1)} %param.34, f32[334,1152]{1,0:T(8,128)S(1)} %get-tuple-element.123, f32[1152]{0:T(1024)S(1)} %copy-done.49, f32[1152]{0:T(1024)S(1)} %copy-done.31, ...), kind=kOutput, calls=%fused_computation.28 | convolution fusion | flops 3649524480 | bytes 27576944 | tf_op jit(solution)/shard_map/dot_general | solution.py:121
  155.9 15.5 %multiply_reduce_fusion.1 = (bf16[4608]{0:T(1024)(128)(2,1)}, bf16[334,4608]{1,0:T(8,128)(2,1)S(1)}) fusion(bf16[334]{0:T(512)(128)(2,1)S(1)} %pad_convert_fusion, f32[334,4608]{1,0:T(8,128)} %get-tuple-element.107, f32[334,4608]{1,0:T(8,128)} %get-tuple-element.124, bf16[4608,1152]{1,0:T(8,128)(2,1)} %param.36, bf16[256,1,1152]{2,0,1:T(8,128)(2,1)S(1)} %copy-done.16, ...), kind=kOutput, calls=%fused_computation.53 | convolution fusion | flops 3572181504 | bytes 26786972 | tf_op jit(solution)/shard_map/dot_general | solution.py:27
  171.4 10.3 multiply_reduce_fusion.3
  187.6 28.6 %multiply_convert_fusion = bf16[16,334,1102]{2,1,0:T(8,128)(2,1)} fusion(f32[16,334,1102]{2,1,0:T(8,128)} %get-tuple-element.121, f32[16,334]{1,0:T(8,128)} %log_add_fusion, bf16[334,16,72]{0,2,1:T(8,128)(2,1)S(1)} %bitcast.158, bf16[1102,16,72]{0,2,1:T(8,128)(2,1)} %bitcast.162), kind=kOutput, calls=%fused_computation.1 | convolution fusion | flops 1737287168 | bytes 38664448 | tf_op jit(solution)/shard_map/sub | solution.py:168
  216.2 18.6 %multiply_bitcast_fusion = (bf16[1,16,334,1102]{3,2,1,0:T(8,128)(2,1)}, bf16[1,16,334,1102]{3,2,1,0:T(8,128)(2,1)S(1)}) fusion(bf16[16,334,1102]{2,1,0:T(8,128)(2,1)} %multiply_convert_fusion, bf16[334]{0:T(512)(128)(2,1)S(1)} %pad_convert_fusion, f32[16,334,1102]{2,1,0:T(8,128)} %get-tuple-element.121, f32[16,334]{1,0:T(8,128)S(1)} %copy-done.27), kind=kLoop, calls=%fused_computation.15 | loop fusion | flops 23556352 | bytes 58912924 | tf_op jit(solution)/shard_map/mul | solution.py:171
  234.8 12.8 %fusion.24 = bf16[16,72,1024]{2,1,0:T(8,128)(2,1)S(1)} fusion(bf16[334,16,72]{0,2,1:T(8,128)(2,1)S(1)} %bitcast.151, bf16[1,16,334,1102]{3,2,1,0:T(8,128)(2,1)} %get-tuple-element.116), kind=kOutput, calls=%fused_computation.60 | convolution fusion | flops 789184512 | bytes 14138880 | tf_op jit(solution)/shard_map/bhqk,qbhd->kbhd/dot_general | solution.py:192
  247.6 4.1 fusion.25
  251.7 2.8 pad_maximum_fusion
  254.6 2.6 fusion.31
  259.9 10.7 %convolution_convert_fusion.1 = bf16[1152,4608]{1,0:T(8,128)(2,1)} fusion(bf16[334,4608]{1,0:T(8,128)(2,1)} %copy-done.55, bf16[334]{0:T(512)(128)(2,1)S(1)} %pad_convert_fusion, f32[334,1152]{1,0:T(8,128)S(1)} %copy-done.9, f32[1152]{0:T(1024)S(1)} %copy-done.50, f32[1152]{0:T(1024)S(1)} %copy-done.31, f32[334]{0:T(512)S(1)} %copy-done.37, ...), kind=kOutput, calls=%fused_computation.10 | convolution fusion | flops 3554793216 | bytes 15246604 | tf_op jit(solution)/shard_map/dot_general | solution.py:21
  271.9 11.0 %convolution_convert_fusion = bf16[4608,1152]{1,0:T(8,128)(2,1)} fusion(bf16[334,4608]{1,0:T(8,128)(2,1)} %get-tuple-element.106, bf16[334]{0:T(512)(128)(2,1)S(1)} %pad_convert_fusion, bf16[256,1,1152]{2,0,1:T(8,128)(2,1)S(1)} %copy-done.17, bf16[78,1,1152]{2,0,1:T(8,128)(2,1)S(1)} %copy-done.24), kind=kOutput, calls=%fused_computation.9 | convolution fusion | flops 3554408448 | bytes 14465180 | tf_op jit(solution)/shard_map/dot_general | solution.py:21
  282.9 5.1 convolution_convert_fusion.4
  288.4 9.1 convolution_convert_fusion.7
  297.5 14.3 %reduce-scatter.22.cloned.1.call-done = bf16[256,1,2304]{0,2,1:T(8,128)(2,1)} async-done(((bf16[1024,1,2304]{0,2,1:T(8,128)(2,1)}), bf16[256,1,2304]{0,2,1:T(8,128)(2,1)}) %reduce-scatter.22.cloned.1.call-update) | async-done | bytes 1179664 | tf_op jit(solution)/shard_map/reduce_scatter | solution.py:196
  313.9 47.7 %all-reduce.14.cloned.1.call-done = (bf16[78,1,1152]{0,2,1:T(8,128)(2,1)}, bf16[78,1,1152]{0,2,1:T(8,128)(2,1)}) async-done(((bf16[78,1,1152]{0,2,1:T(8,128)(2,1)}, bf16[78,1,1152]{0,2,1:T(8,128)(2,1)}), (bf16[78,1,1152]{0,2,1:T(8,128)(2,1)}, bf16[78,1,1152]{0,2,1:T(8,128)(2,1)})) %all-reduce.14.cloned.1.call-update) | async-done | bytes 359440 | tf_op jit(solution)/shard_map/psum | solution.py:187
  361.6 9.1 multiply_reduce_fusion.5
  372.2 7.0 convolution_convert_fusion.3
  379.3 95.3 %reduce-scatter.30.cloned.1.call-done = bf16[144,4608]{1,0:T(8,128)(2,1)} async-done(((bf16[1152,4608]{1,0:T(8,128)(2,1)}), bf16[144,4608]{1,0:T(8,128)(2,1)}) %reduce-scatter.30.cloned.1.call-update) | async-done | bytes 1327120 | tf_op jit(solution)/shard_map/reduce_scatter | solution.py:241
  474.5 3.8 copy.97
  478.4 107.3 %reduce-scatter.32.cloned.1.call-done = bf16[576,1152]{1,0:T(8,128)(2,1)} async-done(((bf16[4608,1152]{1,0:T(8,128)(2,1)}), bf16[576,1152]{1,0:T(8,128)(2,1)}) %reduce-scatter.32.cloned.1.call-update) | async-done | bytes 1327120 | tf_op jit(solution)/shard_map/reduce_scatter | solution.py:241
  588.8 36.1 %reduce-scatter.28.cloned.1.call-done = bf16[144,1152]{1,0:T(8,128)(2,1)} async-done(((bf16[1152,1152]{1,0:T(8,128)(2,1)}), bf16[144,1152]{1,0:T(8,128)(2,1)}) %reduce-scatter.28.cloned.1.call-update) | async-done | bytes 331792 | tf_op jit(solution)/shard_map/reduce_scatter | solution.py:241
  627.1 9.2 convolution_convert_fusion.2
  636.4 50.3 %reduce-scatter.24.cloned.1.call-done = bf16[288,1152]{1,0:T(8,128)(2,1)} async-done(((bf16[2304,1152]{1,0:T(8,128)(2,1)}), bf16[288,1152]{1,0:T(8,128)(2,1)}) %reduce-scatter.24.cloned.1.call-update) | async-done | bytes 663568 | tf_op jit(solution)/shard_map/reduce_scatter | solution.py:241
  689.1 37.3 %reduce-scatter.40.cloned.1.call-done = bf16[1152,144]{1,0:T(8,128)(2,1)} async-done(((bf16[4608,144]{1,0:T(8,128)(2,1)}), bf16[1152,144]{1,0:T(8,128)(2,1)}) %reduce-scatter.40.cloned.1.call-update) | async-done | bytes 331792
  730.4 29.6 %reduce-scatter.42.cloned.1.call-done = bf16[288,576]{1,0:T(8,128)(2,1)} async-done(((bf16[1152,576]{1,0:T(8,128)(2,1)}), bf16[288,576]{1,0:T(8,128)(2,1)}) %reduce-scatter.42.cloned.1.call-update) | async-done | bytes 331792
  760.1 9.2 fusion.19
  772.7 15.6 %reduce-scatter.38.cloned.1.call-done = bf16[288,144]{1,0:T(8,128)(2,1)} async-done(((bf16[1152,144]{1,0:T(8,128)(2,1)}), bf16[288,144]{1,0:T(8,128)(2,1)}) %reduce-scatter.38.cloned.1.call-update) | async-done | bytes 82960
  789.4 9.9 all-gather.1
  800.7 6.3 convolution_bitcast_fusion
  807.0 69.6 %reduce-scatter.26.cloned.1.call-done = bf16[144,3456]{1,0:T(8,128)(2,1)} async-done(((bf16[1152,3456]{1,0:T(8,128)(2,1)}), bf16[144,3456]{1,0:T(8,128)(2,1)}) %reduce-scatter.26.cloned.1.call-update) | async-done | bytes 995344 | tf_op jit(solution)/shard_map/reduce_scatter | solution.py:241
  888.9 26.4 %all-reduce.10 = (bf16[1152]{0:T(1024)(128)(2,1)S(1)}, bf16[1152]{0:T(1024)(128)(2,1)S(1)}, bf16[1152]{0:T(1024)(128)(2,1)S(1)}, bf16[1152]{0:T(1024)(128)(2,1)S...) all-reduce(bf16[1152]{0:T(1024)(128)(2,1)S(1)} %get-tuple-element.8, ...), channel_id=5, replica_groups=mesh['batch'=8,'seq'=4] {'batch'}, use_global_device_ids=true, to_apply=%region_17.18.clone | all-reduce | flops 12672 | bytes 50688
  916.0 16.6 %all-reduce.9 = (f32[144]{0:T(256)}, f32[144]{0:T(256)}, f32[144]{0:T(256)}, f32[144]{0:T(256)}, f32[144]{0:T(256)}, /*index=5*/f32[144]{0:T(256)}, f32[576]{0:T(1024)}, f32[144]{0:T(256)}) all-reduce(f32[144]{0:T(256)S(1)} %dynamic-slice_convert_fusion.7, ...), channel_id=1, replica_groups=mesh['batch'=8,'seq'=4] {'seq'}, use_global_device_ids=true, to_apply=%region_18.19 | all-reduce | flops 1584 | bytes 12672 | tf_op jit(solution)/shard_map/psum | solution.py:262
  932.6 12.8 %all_gather.20 = bf16[288,1152]{0,1:T(8,128)(2,1)S(1)} all-gather(bf16[288,288]{0,1:T(8,128)(2,1)} %bitcast.178), channel_id=1, replica_groups=mesh['batch'=8,'seq'=4] {'seq'}, dimensions={1}, use_global_device_ids=true | all-gather | bytes 829440 | tf_op jit(solution)/shard_map/all_gather | solution.py:276
  946.8 3.1 convert_element_type.250
  949.8 22.8 %all-gather.10.cloned.1.call-done = bf16[576,1152]{0,1:T(8,128)(2,1)} async-done(((bf16[576,288]{0,1:T(8,128)(2,1)}), bf16[576,1152]{0,1:T(8,128)(2,1)}) %all-gather.10.cloned.1.call-update) | async-done | bytes 1327120 | tf_op jit(solution)/shard_map/all_gather | solution.py:288
  972.6 2.9 copy.88
  975.5 33.0 %reduce-scatter.36.cloned.1.call-done = bf16[864,144]{1,0:T(8,128)(2,1)} async-done(((bf16[3456,144]{1,0:T(8,128)(2,1)}), bf16[864,144]{1,0:T(8,128)(2,1)}) %reduce-scatter.36.cloned.1.call-update) | async-done | bytes 248848
  1009.8 13.7 %all-gather = bf16[4,864,144]{1,2,0:T(8,128)(2,1)S(1)} all-gather(bf16[1,864,144]{1,2,0:T(8,128)(2,1)S(1)} %bitcast.166), channel_id=1, replica_groups=mesh['batch'=8,'seq'=4] {'seq'}, dimensions={0}, use_global_device_ids=true | all-gather | bytes 1244160 | tf_op jit(solution)/shard_map/all_gather | solution.py:279
  1025.2 3.2 reshape.369
  (199 shorter events, 59.0 us)
Async XLA Ops:
  7.2 124.6 %copy-start = (bf16[1152,1152]{1,0:T(8,128)(2,1)S(1)}, bf16[1152,1152]{1,0:T(8,128)(2,1)}, u32[]{:S(2)}) copy-start(bf16[1152,1152]{1,0:T(8,128)(2,1)} %param.30) | copy-start | bytes 7962628
  7.2 5.8 copy-start.32
  7.2 5.8 copy-start.51
  7.2 72.3 %all-gather.6.cloned.1.call-start = ((), (), s32[]{:S(2)}) async-start(), calls=%async_computation.11 | async-start | bytes 5898240 | tf_op jit(solution)/shard_map/all_gather | solution.py:89
  19.6 292.1 %reduce-scatter.22.cloned.1.call-start = ((), (), s32[]{:S(2)}) async-start(), calls=%async_computation.12 | async-start | bytes 5898240 | tf_op jit(solution)/shard_map/reduce_scatter | solution.py:196
  26.1 68.7 %copy-start.6 = (bf16[334,1,1152]{0,2,1:T(8,128)(2,1)}, bf16[334,1,1152]{0,2,1:T(8,128)(2,1)S(1)}, u32[]{:S(2)}) copy-start(bf16[334,1,1152]{0,2,1:T(8,128)(2,1)S(1)} %copy.72) | copy-start | bytes 2308612
  109.1 12.1 %copy-start.15 = (bf16[1102,1,1152]{0,2,1:T(8,128)(2,1)S(1)}, bf16[1102,1,1152]{0,2,1:T(8,128)(2,1)}, u32[]{:S(2)}) copy-start(bf16[1102,1,1152]{0,2,1:T(8,128)(2,1)} %copy.71) | copy-start | bytes 7617028
  121.2 10.5 %copy-start.12 = (f32[334,1152]{1,0:T(8,128)S(1)}, f32[334,1152]{1,0:T(8,128)}, u32[]{:S(2)}) copy-start(f32[334,1152]{1,0:T(8,128)} %copy-done.11) | copy-start | bytes 4617220
  121.2 10.6 %copy-start.48 = (f32[1152]{0:T(1024)S(1)}, f32[1152]{0:T(1024)}, u32[]{:S(2)}) copy-start(f32[1152]{0:T(1024)} %param.31) | copy-start | bytes 13828
  133.3 48.4 %copy-start.8 = (f32[334,1152]{1,0:T(8,128)}, f32[334,1152]{1,0:T(8,128)S(1)}, u32[]{:S(2)}) copy-start(f32[334,1152]{1,0:T(8,128)S(1)} %get-tuple-element.123) | copy-start | bytes 4617220
  133.7 48.1 %copy-start.36 = (f32[334]{0:T(512)}, f32[334]{0:T(512)S(1)}, u32[]{:S(2)}) copy-start(f32[334]{0:T(512)S(1)} %add_rsqrt_fusion) | copy-start | bytes 4012
  133.7 22.2 %copy-start.16 = (bf16[256,1,1152]{2,0,1:T(8,128)(2,1)S(1)}, bf16[256,1,1152]{2,0,1:T(8,128)(2,1)}, u32[]{:S(2)}) copy-start(bf16[256,1,1152]{2,0,1:T(8,128)(2,1)} %param.38) | copy-start | bytes 1769476
  133.7 22.2 %copy-start.23 = (bf16[78,1,1152]{2,0,1:T(8,128)(2,1)S(1)}, bf16[78,1,1152]{2,0,1:T(8,128)(2,1)}, u32[]{:S(2)}) copy-start(bf16[78,1,1152]{2,0,1:T(8,128)(2,1)} %param.39) | copy-start | bytes 539140
  155.9 15.6 %copy-start.40 = (f32[334]{0:T(512)S(1)}, f32[334]{0:T(512)}, u32[]{:S(2)}) copy-start(f32[334]{0:T(512)} %concatenate.71) | copy-start | bytes 4012
  171.4 10.3 copy-start.55
  187.6 28.6 %copy-start.27 = (f32[16,334]{1,0:T(8,128)S(1)}, f32[16,334]{1,0:T(8,128)}, u32[]{:S(2)}) copy-start(f32[16,334]{1,0:T(8,128)} %log_add_fusion) | copy-start | bytes 64132
  216.2 18.6 %copy-start.7 = (bf16[334,1,1152]{0,2,1:T(8,128)(2,1)S(1)}, bf16[334,1,1152]{0,2,1:T(8,128)(2,1)}, u32[]{:S(2)}) copy-start(bf16[334,1,1152]{0,2,1:T(8,128)(2,1)} %copy-done.6) | copy-start | bytes 2308612
  234.8 12.8 %copy-start.2 = (bf16[1,16,334,1102]{3,2,1,0:T(8,128)(2,1)}, bf16[1,16,334,1102]{3,2,1,0:T(8,128)(2,1)S(1)}, u32[]{:S(2)}) copy-start(bf16[1,16,334,1102]{3,2,1,0:T(8,128)(2,1)S(1)} %get-tuple-element.117) | copy-start | bytes 35334532
  254.6 107.0 %all-reduce.14.cloned.1.call-start = ((), (), s32[]{:S(2)}) async-start(), calls=%async_computation.25 | async-start | bytes 1179648 | tf_op jit(solution)/shard_map/psum | solution.py:187
  259.8 214.7 %reduce-scatter.30.cloned.1.call-start = ((), (), s32[]{:S(2)}) async-start(), calls=%async_computation.16 | async-start | bytes 11943936 | tf_op jit(solution)/shard_map/reduce_scatter | solution.py:241
  270.7 315.1 %reduce-scatter.32.cloned.1.call-start = ((), (), s32[]{:S(2)}) async-start(), calls=%async_computation.18 | async-start | bytes 11943936 | tf_op jit(solution)/shard_map/reduce_scatter | solution.py:241
  282.9 342.0 %reduce-scatter.28.cloned.1.call-start = ((), (), s32[]{:S(2)}) async-start(), calls=%async_computation.15 | async-start | bytes 2985984 | tf_op jit(solution)/shard_map/reduce_scatter | solution.py:241
  288.1 73.5 %copy-start.29 = (f32[334]{0:T(512)S(1)}, f32[334]{0:T(512)}, u32[]{:S(2)}) copy-start(f32[334]{0:T(512)} %copy-done.28) | copy-start | bytes 4012
  288.1 73.5 %copy-start.33 = (f32[1152]{0:T(1024)S(1)}, f32[1152]{0:T(1024)}, u32[]{:S(2)}) copy-start(f32[1152]{0:T(1024)} %param.27) | copy-start | bytes 13828
  288.1 73.5 %copy-start.35 = (f32[334]{0:T(512)S(1)}, f32[334]{0:T(512)}, u32[]{:S(2)}) copy-start(f32[334]{0:T(512)} %copy-done.34) | copy-start | bytes 4012
  288.1 73.5 %copy-start.41 = (f32[334]{0:T(512)S(1)}, f32[334]{0:T(512)}, u32[]{:S(2)}) copy-start(f32[334]{0:T(512)} %concatenate.71) | copy-start | bytes 4012
  288.1 398.6 %reduce-scatter.24.cloned.1.call-start = ((), (), s32[]{:S(2)}) async-start(), calls=%async_computation.13 | async-start | bytes 5971968 | tf_op jit(solution)/shard_map/reduce_scatter | solution.py:241
  313.9 56.8 %copy-start.25 = (bf16[256,1,1152]{0,2,1:T(8,128)(2,1)}, bf16[256,1,1152]{0,2,1:T(8,128)(2,1)S(1)}, u32[]{:S(2)}) copy-start(bf16[256,1,1152]{0,2,1:T(8,128)(2,1)S(1)} %get-tuple-element.114) | copy-start | bytes 1769476
  361.6 9.2 copy-start.5
  361.6 9.2 copy-start.13
  371.8 7.4 copy-start.21
  379.2 347.2 %reduce-scatter.40.cloned.1.call-start = ((), (), s32[]{:S(2)}) async-start(), calls=%async_computation.23 | async-start | bytes 2949120
  478.3 148.7 %copy-start.14 = (f32[334,1152]{1,0:T(8,128)S(1)}, f32[334,1152]{1,0:T(8,128)}, u32[]{:S(2)}) copy-start(f32[334,1152]{1,0:T(8,128)} %copy-done.11) | copy-start | bytes 4617220
  478.3 148.7 %copy-start.20 = (bf16[16,72,334]{2,1,0:T(8,128)(2,1)S(1)}, bf16[16,72,334]{2,1,0:T(8,128)(2,1)}, u32[]{:S(2)}) copy-start(bf16[16,72,334]{2,1,0:T(8,128)(2,1)} %convolution_convert_fusion.7) | copy-start | bytes 2308612
  478.4 148.7 %copy-start.26 = (bf16[256,1,1152]{0,2,1:T(8,128)(2,1)S(1)}, bf16[256,1,1152]{0,2,1:T(8,128)(2,1)}, u32[]{:S(2)}) copy-start(bf16[256,1,1152]{0,2,1:T(8,128)(2,1)} %copy-done.25) | copy-start | bytes 1769476
  478.4 148.7 %copy-start.52 = (f32[1152]{0:T(1024)S(1)}, f32[1152]{0:T(1024)}, u32[]{:S(2)}) copy-start(f32[1152]{0:T(1024)} %param.28) | copy-start | bytes 13828
  478.4 281.6 %reduce-scatter.42.cloned.1.call-start = ((), (), s32[]{:S(2)}) async-start(), calls=%async_computation.24 | async-start | bytes 1843200
  588.4 200.0 %reduce-scatter.38.cloned.1.call-start = ((), (), s32[]{:S(2)}) async-start(), calls=%async_computation.22 | async-start | bytes 737280
  627.0 249.7 %reduce-scatter.26.cloned.1.call-start = ((), (), s32[]{:S(2)}) async-start(), calls=%async_computation.14 | async-start | bytes 8957952 | tf_op jit(solution)/shard_map/reduce_scatter | solution.py:241
  636.3 92.2 %copy-start.54 = (u32[32]{0:T(128)S(1)}, u32[32]{0:T(128)}, u32[]{:S(2)}) copy-start(u32[32]{0:T(128)} %constant.106) | copy-start | bytes 388
  636.3 123.7 %copy-start.10 = (f32[334,1152]{1,0:T(8,128)S(1)}, f32[334,1152]{1,0:T(8,128)}, u32[]{:S(2)}) copy-start(f32[334,1152]{1,0:T(8,128)} %copy-done.8) | copy-start | bytes 4617220
  636.4 123.7 %copy-start.53 = (f32[1152]{0:T(1024)S(1)}, f32[1152]{0:T(1024)}, u32[]{:S(2)}) copy-start(f32[1152]{0:T(1024)} %param.37) | copy-start | bytes 13828
  636.4 296.2 %reduce-scatter.34.cloned.1.call-start = ((), (), s32[]{:S(2)}) async-start(), calls=%async_computation.20 | async-start | bytes 1105920
  689.0 257.7 %all-gather.8.cloned.1.call-start = ((), (), s32[]{:S(2)}) async-start(), calls=%async_computation.17 | async-start | bytes 1658880 | tf_op jit(solution)/shard_map/all_gather | solution.py:285
  728.4 244.2 %all-gather.10.cloned.1.call-start = ((), (), s32[]{:S(2)}) async-start(), calls=%async_computation.19 | async-start | bytes 1843200 | tf_op jit(solution)/shard_map/all_gather | solution.py:288
  760.0 248.6 %reduce-scatter.36.cloned.1.call-start = ((), (), s32[]{:S(2)}) async-start(), calls=%async_computation.21 | async-start | bytes 2211840
  770.5 30.2 %copy-start.22 = (bf16[334,1152]{1,0:T(8,128)(2,1)S(1)}, bf16[334,1152]{1,0:T(8,128)(2,1)}, u32[]{:S(2)}) copy-start(bf16[334,1152]{1,0:T(8,128)(2,1)} %copy-done.21) | copy-start | bytes 2308612
  1009.8 18.6 %copy-start.1 = (bf16[1152,1152]{1,0:T(8,128)(2,1)S(1)}, bf16[1152,1152]{1,0:T(8,128)(2,1)}, u32[]{:S(2)}) copy-start(bf16[1152,1152]{1,0:T(8,128)(2,1)} %param.30) | copy-start | bytes 7962628
  (23 other events, 73.4 us)
Sparse Core Ops, SparseCore 0:
  19.8 59.7 all-gather.5
  254.7 57.0 reduce-scatter.21
  315.4 46.1 all-reduce.13
  363.9 110.6 reduce-scatter.29
  476.7 109.0 reduce-scatter.31
  588.6 36.2 reduce-scatter.27
  627.3 59.3 reduce-scatter.23
  690.6 35.7 reduce-scatter.39
  729.7 30.2 reduce-scatter.41
  763.3 25.0 reduce-scatter.37
  790.8 85.8 reduce-scatter.25
  880.0 25.0 reduce-scatter.33
  907.5 31.9 all-gather.7
  941.2 31.3 all-gather.9
  976.1 32.4 reduce-scatter.35
where the time goes:
time: 1040 us
  waiting for transfers between devices  612 us (59%)
  matrix products  213 us (20%)
  blocking collectives  79.4 us (8%)
  local copies, waits for them, and re-layouts  67.8 us (7%)
  other arithmetic  44.5 us (4%)
  between operations  16.9 us (2%)
    reduce_scatter x5, waiting for transfers between devices, per_device(): lax.psum_scatter(shortened(rest_grads + mlp_grads), 'batch', scatter_dime...  359 us
    unnamed x20, waiting for transfers between devices  116 us
    all_gather x1, waiting for transfers between devices, per_device(): lax.all_gather(local_pairs[cond_rows:], 'seq', axis=0, tiled=True)  52.8 us
    psum x1, waiting for transfers between devices, per_device(): lax.psum(cond_vals.astype(jnp.bfloat16), 'seq').astype(jnp.float32)  47.7 us
    dot_general x5, matrix products, times_transpose(): lax.dot_general(left, right, (((1,), (1,)), ((), ())), preferred_element_...  43.5 us
    dot_general x5, matrix products, contract_rows(): lax.dot_general(left, right, (((0,), (0,)), ((), ())), preferred_element_...  43.2 us
    unnamed x129, local copies, waits for them, and re-layouts  36.6 us
    sub x1, matrix products, per_device(): d_probs - row_delta  28.6 us
  transfers between devices with their start and end apart: 15, of which 13 were waited for; matrix products, arithmetic and copies ran while one was open for 13% of the time, Pallas kernels for 0%

commit v1 on v0

v1 whole, which is shorter than its diff:
```python
import functools
import math

import jax
import jax.numpy as jnp
from jax import lax
from jax.experimental import pallas as pl
from jax.experimental.pallas import tpu as pltpu
from jax.sharding import PartitionSpec as P

HEADS = 16
HEAD_DIM = 72
LANES = 128
SLOTS = 128
F32 = jnp.float32
BF16 = jnp.bfloat16
VMEM_LIMIT = 60 * 1024 * 1024
SCALE = 1.0 / math.sqrt(HEAD_DIM)
SCALE2 = SCALE * math.log2(math.e)


def dot(left, right):
    return jnp.dot(left, right, preferred_element_type=F32)


def dot_nt(left, right):
    return lax.dot_general(left, right, (((1,), (1,)), ((), ())), preferred_element_type=F32)


def dot_tn(left, right):
    return lax.dot_general(left, right, (((0,), (0,)), ((), ())), preferred_element_type=F32)


def params():
    return pltpu.CompilerParams(vmem_limit_bytes=VMEM_LIMIT)


def cost(flops, nbytes):
    return pl.CostEstimate(flops=int(flops), bytes_accessed=int(nbytes), transcendentals=0)


def turned(value):
    return value.astype(F32).T.astype(BF16)


def normalize(values):
    centre = values - jnp.mean(values, axis=-1, keepdims=True)
    factor = lax.rsqrt(jnp.mean(centre * centre, axis=-1, keepdims=True) + 1e-5)
    return centre * factor, factor


def norm_back(upstream, scaled, factor, gain):
    inner = upstream * gain
    centred = inner - jnp.mean(inner, axis=-1, keepdims=True)
    return factor * (centred - scaled * jnp.mean(inner * scaled, axis=-1, keepdims=True))


def pre_kernel(x_ref, s_ref, w_ref, bias_ref, gain_ref, shift_ref, hidden_ref, normed_ref, turn_ref):
    width = x_ref.shape[1]
    hidden = dot(x_ref[...], w_ref[:width]) + dot(s_ref[...], w_ref[width:]) + bias_ref[...]
    hidden_ref[...] = hidden
    scaled, _ = normalize(hidden)
    normed_ref[...] = (scaled * gain_ref[...] + shift_ref[...]).astype(BF16)
    turn_ref[:width] = turned(x_ref[...])
    turn_ref[width:] = turned(s_ref[...])


def pre(x, s, w, bias, gain, shift):
    rows, width = x.shape
    return pl.pallas_call(
        pre_kernel,
        out_shape=(
            jax.ShapeDtypeStruct((rows, width), F32),
            jax.ShapeDtypeStruct((rows, width), BF16),
            jax.ShapeDtypeStruct((2 * width, rows), BF16),
        ),
        compiler_params=params(),
        cost_estimate=cost(4 * rows * width * width, 4 * width * width + 12 * rows * width),
        name="input_linear",
    )(x, s, w, bias, gain, shift)


def heads_weight_kernel(window, place_ref, w_ref, out_ref):
    heads = out_ref.shape[0]
    width = w_ref.shape[0]
    own = heads * HEAD_DIM
    keep = lax.broadcasted_iota(jnp.int32, (width, LANES), 1) < HEAD_DIM
    place = place_ref[0]
    for which in range(3):
        first = place * own + which * width
        start = jnp.minimum(first // LANES * LANES, 3 * width - window)
        value = w_ref[:, pl.ds(pl.multiple_of(start, LANES), window)].astype(F32)
        value = pltpu.roll(value, lax.rem(window - (first - start), window), 1)
        for head in range(heads):
            turned_back = value if head == 0 else pltpu.roll(value, window - head * HEAD_DIM, 1)
            out_ref[head, :, which * LANES : (which + 1) * LANES] = jnp.where(
                keep, turned_back[:, :LANES], 0.0
            ).astype(BF16)


def heads_weight(place, w, heads):
    width = w.shape[0]
    own = heads * HEAD_DIM
    offsets = [p * own % LANES for p in range(HEADS // heads)]
    window = (max(offsets) + own + LANES - 1) // LANES * LANES
    return pl.pallas_call(
        functools.partial(heads_weight_kernel, window),
        in_specs=[
            pl.BlockSpec(memory_space=pltpu.SMEM),
            pl.BlockSpec(memory_space=pltpu.VMEM),
        ],
        out_shape=jax.ShapeDtypeStruct((heads, width, 3 * LANES), BF16),
        compiler_params=params(),
        cost_estimate=cost(1e6, 2 * w.size + 6 * heads * width * LANES),
        name="heads_weight",
    )(place, w)


def attend_kernel(parts, normed_ref, w_ref, kbias_ref, qkv_ref, lse_ref, *rest):
    ctx_refs, (vt_ref, ot_ref) = rest[:parts], rest[parts:]
    head = pl.program_id(0)
    total = normed_ref.shape[0]
    rows = total // parts
    lane = lax.broadcasted_iota(jnp.int32, (1, LANES), 1)
    one = jnp.where(lane == HEAD_DIM, 1.0, 0.0)
    for part in range(parts):
        span = pl.ds(part * rows, rows)
        triple = dot(normed_ref[span], w_ref[0])
        qkv_ref[0, span, :LANES] = (triple[:, :LANES] + one).astype(BF16)
        qkv_ref[0, span, LANES : 2 * LANES] = (
            triple[:, LANES : 2 * LANES] + kbias_ref[span]
        ).astype(BF16)
        qkv_ref[0, span, 2 * LANES :] = triple[:, 2 * LANES :].astype(BF16)
        vt_ref[:, span] = turned(qkv_ref[0, span, 2 * LANES :])
    step = 3 * LANES if total % (3 * LANES) == 0 else LANES
    for start in range(0, total, step):
        query = qkv_ref[0, pl.ds(start, step), :LANES]
        scores = dot_nt(qkv_ref[0, :, LANES : 2 * LANES], query)
        peak = jnp.max(scores, axis=0, keepdims=True)
        shifted = jnp.exp2((scores - peak) * SCALE2)
        sums = jnp.sum(shifted, axis=0, keepdims=True)
        mixed = dot(vt_ref[...], shifted.astype(BF16)) / sums
        ot_ref[pl.ds(pl.multiple_of(head * HEAD_DIM, 8), HEAD_DIM), pl.ds(start, step)] = mixed[
            :HEAD_DIM
        ]
        lse_ref[0, :, pl.ds(start, step)] = peak * SCALE2 + jnp.log2(sums)

    @pl.when(head == pl.num_programs(0) - 1)
    def _():
        for part in range(parts):
            ctx_refs[part][...] = ot_ref[:, pl.ds(part * rows, rows)].T.astype(BF16)


def attend(parts, normed_all, w_heads, kbias):
    total, width = normed_all.shape
    heads = w_heads.shape[0]
    rows = total // parts
    own = heads * HEAD_DIM
    return pl.pallas_call(
        functools.partial(attend_kernel, parts),
        grid=(heads,),
        in_specs=[
            pl.BlockSpec((total, width), lambda h: (0, 0)),
            pl.BlockSpec((1, width, 3 * LANES), lambda h: (h, 0, 0)),
            pl.BlockSpec((total, LANES), lambda h: (0, 0)),
        ],
        out_specs=[
            pl.BlockSpec((1, total, 3 * LANES), lambda h: (h, 0, 0)),
            pl.BlockSpec((1, 1, total), lambda h: (h, 0, 0)),
        ]
        + [pl.BlockSpec((rows, own), lambda h: (0, 0))] * parts,
        out_shape=[
            jax.ShapeDtypeStruct((heads, total, 3 * LANES), BF16),
            jax.ShapeDtypeStruct((heads, 1, total), F32),
        ]
        + [jax.ShapeDtypeStruct((rows, own), BF16)] * parts,
        scratch_shapes=[pltpu.VMEM((LANES, total), BF16), pltpu.VMEM((own, total), F32)],
        compiler_params=params(),
        cost_estimate=cost(
            2 * heads * total * (width * 3 * LANES + 4 * LANES * total), 6 * total * width
        ),
        name="attend",
    )(normed_all, w_heads, kbias)


def attend_back_kernel(parts, *refs):
    d_refs = refs[:parts]
    (qkv_ref, lse_ref, w_ref, dt_ref, lead_ref, tail_ref) = refs[parts : parts + 6]
    (dot_all, dt_all, acc, dq_ref, dk_ref, dv_ref) = refs[parts + 6 :]
    head = pl.program_id(0)
    heads = pl.num_programs(0)
    total = qkv_ref.shape[1]
    rows = total // parts
    half = rows // 2
    own = dot_all.shape[0]

    @pl.when(head == 0)
    def _():
        for part in range(parts):
            dot_all[:, pl.ds(part * rows, rows)] = d_refs[part][...].astype(F32).T

    base = pl.multiple_of(head * HEAD_DIM, 8)
    upstream_t = jnp.concatenate(
        [dot_all[pl.ds(base, HEAD_DIM), :], jnp.zeros((LANES - HEAD_DIM, total), F32)], 0
    )
    upstream = upstream_t.T.astype(BF16)
    upstream_t = upstream_t.astype(BF16)
    key = qkv_ref[0, :, LANES : 2 * LANES]
    key_t = turned(key)
    value = qkv_ref[0, :, 2 * LANES :]
    step = 3 * LANES if total % (3 * LANES) == 0 else LANES
    for start in range(0, total, step):
        query = qkv_ref[0, pl.ds(start, step), :LANES]
        probs = jnp.exp2(dot_nt(key, query) * SCALE2 - lse_ref[0, :, pl.ds(start, step)])
        d_probs = dot(value, upstream_t[:, start : start + step])
        delta = jnp.sum(probs * d_probs, axis=0, keepdims=True)
        d_raw = (probs * (d_probs - delta) * SCALE).astype(BF16)
        d_value = dot(probs.astype(BF16), upstream[start : start + step])
        d_key = dot(d_raw, query)
        if start == 0:
            dv_ref[...] = d_value
            dk_ref[...] = d_key
        else:
            dv_ref[...] += d_value
            dk_ref[...] += d_key
        d_query = dot(key_t, d_raw)
        dt_all[pl.ds(base, HEAD_DIM), pl.ds(start, step)] = d_query[:HEAD_DIM]
        dq_ref[pl.ds(start, step)] = d_query.T
    dt_all[pl.ds(pl.multiple_of(own + base, 8), HEAD_DIM)] = dk_ref[...].T[:HEAD_DIM]
    dt_all[pl.ds(pl.multiple_of(2 * own + base, 8), HEAD_DIM)] = dv_ref[...].T[:HEAD_DIM]
    for part in range(parts):
        span = pl.ds(part * rows, rows)
        update = (
            dot_nt(dq_ref[span].astype(BF16), w_ref[0, :, :LANES])
            + dot_nt(dk_ref[span].astype(BF16), w_ref[0, :, LANES : 2 * LANES])
            + dot_nt(dv_ref[span].astype(BF16), w_ref[0, :, 2 * LANES :])
        )

        @pl.when(head == 0)
        def _():
            acc[span] = update

        @pl.when(head > 0)
        def _():
            acc[span] += update

    @pl.when(head == heads - 1)
    def _():
        dt_ref[...] = dt_all[...].astype(BF16)
        for part in range(parts):
            lead_ref[part] = acc[pl.ds(part * rows, half)].astype(BF16)
            tail_ref[part] = acc[pl.ds(part * rows + half, half)].astype(BF16)


def attend_back(parts, d_context, qkv, lse, w_heads):
    heads, total, _ = qkv.shape
    width = w_heads.shape[1]
    rows = total // parts
    own = heads * HEAD_DIM
    whole = lambda *shape: pl.BlockSpec(shape, lambda h: (0,) * len(shape))
    return pl.pallas_call(
        functools.partial(attend_back_kernel, parts),
        grid=(heads,),
        in_specs=[whole(rows, own)] * parts
        + [
            pl.BlockSpec((1, total, 3 * LANES), lambda h: (h, 0, 0)),
            pl.BlockSpec((1, 1, total), lambda h: (h, 0, 0)),
            pl.BlockSpec((1, width, 3 * LANES), lambda h: (h, 0, 0)),
        ],
        out_specs=[
            whole(3 * own, total),
            whole(parts, rows // 2, width),
            whole(parts, rows // 2, width),
        ],
        out_shape=[
            jax.ShapeDtypeStruct((3 * own, total), BF16),
            jax.ShapeDtypeStruct((parts, rows // 2, width), BF16),
            jax.ShapeDtypeStruct((parts, rows // 2, width), BF16),
        ],
        scratch_shapes=[
            pltpu.VMEM((own, total), F32),
            pltpu.VMEM((3 * own, total), F32),
            pltpu.VMEM((total, width), F32),
            pltpu.VMEM((total, LANES), F32),
            pltpu.VMEM((total, LANES), F32),
            pltpu.VMEM((total, LANES), F32),
        ],
        compiler_params=params(),
        cost_estimate=cost(
            2 * heads * total * (width * 3 * LANES + 10 * LANES * total), 12 * total * width
        ),
        name="attend_back",
    )(*d_context, qkv, lse, w_heads)


def mlp_kernel(parts, place_ref, *refs):
    ctx_refs = refs[:parts]
    (
        hidden_ref,
        cot_ref,
        proj_ref,
        vec_ref,
        fc1_ref,
        fc1_bias_ref,
        fc2_ref,
        out_ref,
        d_middle_ref,
        d_branch_ref,
        active_t_ref,
        d_pre_ref,
        normed_t_ref,
        ctx_t_ref,
        vec_out_ref,
        fc1_bias_out_ref,
    ) = refs[parts : parts + 16]
    d_ctx_refs = refs[parts + 16 : 2 * parts + 16]
    middle_ref, normed_ref, acc_out, acc_back, turn_ref = refs[2 * parts + 16 :]
    step = pl.program_id(0)
    place = place_ref[0]
    own = ctx_refs[0].shape[1]

    @pl.when(step == 0)
    def _():
        branch = vec_ref[0:1] + hidden_ref[...]
        for part in range(parts):
            at = pl.ds(pl.multiple_of((place ^ part) * own, 8), own)
            branch += dot(ctx_refs[part][...], proj_ref[at, :])
            turn_ref[at] = ctx_refs[part][...].astype(F32).T
        ctx_t_ref[...] = turn_ref[...].astype(BF16)
        middle_ref[...] = branch
        scaled, _ = normalize(branch)
        normed = (scaled * vec_ref[1:2] + vec_ref[2:3]).astype(BF16)
        normed_ref[...] = normed
        normed_t_ref[...] = turned(normed)

    before = dot(normed_ref[...], fc1_ref[...]) + fc1_bias_ref[...]
    cdf = 0.5 + 0.5 * lax.erf(before * math.sqrt(0.5))
    active = (before * cdf).astype(BF16)
    slope = cdf + before * (jnp.exp(-0.5 * before * before) * (1.0 / math.sqrt(2.0 * math.pi)))
    d_before = dot_nt(cot_ref[...], fc2_ref[...]) * slope
    fc1_bias_out_ref[...] = jnp.sum(d_before, axis=0, keepdims=True)
    d_low = d_before.astype(BF16)
    d_pre_ref[...] = d_low
    active_t_ref[...] = turned(active)
    forward = dot(active, fc2_ref[...])
    backward = dot_nt(d_low, fc1_ref[...])

    @pl.when(step == 0)
    def _():
        acc_out[...] = forward
        acc_back[...] = backward

    @pl.when(step > 0)
    def _():
        acc_out[...] += forward
        acc_back[...] += backward

    @pl.when(step == pl.num_programs(0) - 1)
    def _():
        middle = middle_ref[...]
        out_ref[...] = middle + acc_out[...] + vec_ref[3:4]
        scaled, factor = normalize(middle)
        upstream = acc_back[...]
        cot = cot_ref[...].astype(F32)
        d_middle = cot + norm_back(upstream, scaled, factor, vec_ref[1:2])
        d_middle_ref[...] = d_middle
        d_branch = d_middle.astype(BF16)
        d_branch_ref[...] = d_branch
        vec_out_ref[0:1] = jnp.sum(upstream * scaled, axis=0, keepdims=True)
        vec_out_ref[1:2] = jnp.sum(upstream, axis=0, keepdims=True)
        vec_out_ref[2:3] = jnp.sum(d_middle, axis=0, keepdims=True)
        vec_out_ref[3:4] = jnp.sum(cot, axis=0, keepdims=True)
        vec_out_ref[4:] = jnp.zeros((4, vec_out_ref.shape[1]), F32)
        for part in range(parts):
            at = pl.ds(pl.multiple_of((place ^ part) * own, 8), own)
            d_ctx_refs[part][...] = dot_nt(d_branch, proj_ref[at, :]).astype(BF16)


def mlp(parts, place, context, hidden, cot, proj, vecs, fc1, fc1_bias, fc2):
    rows, width = hidden.shape
    ff = fc1.shape[1]
    own = context[0].shape[1]
    chunk = width
    whole = lambda *shape: pl.BlockSpec(shape, lambda i, p: (0,) * len(shape))
    return pl.pallas_call(
        functools.partial(mlp_kernel, parts),
        grid_spec=pltpu.PrefetchScalarGridSpec(
            num_scalar_prefetch=1,
            grid=(ff // chunk,),
            in_specs=[whole(rows, own)] * parts
            + [
                whole(rows, width),
                whole(rows, width),
                whole(width, width),
                whole(8, width),
                pl.BlockSpec((width, chunk), lambda i, p: (0, i)),
                pl.BlockSpec((1, chunk), lambda i, p: (0, i)),
                pl.BlockSpec((chunk, width), lambda i, p: (i, 0)),
            ],
            out_specs=[
                whole(rows, width),
                whole(rows, width),
                whole(rows, width),
                pl.BlockSpec((chunk, rows), lambda i, p: (i, 0)),
                pl.BlockSpec((rows, chunk), lambda i, p: (0, i)),
                whole(width, rows),
                whole(width, rows),
                whole(8, width),
                pl.BlockSpec((1, chunk), lambda i, p: (0, i)),
            ]
            + [whole(rows, own)] * parts,
            scratch_shapes=[
                pltpu.VMEM((rows, width), F32),
                pltpu.VMEM((rows, width), BF16),
                pltpu.VMEM((rows, width), F32),
                pltpu.VMEM((rows, width), F32),
                pltpu.VMEM((width, rows), F32),
            ],
        ),
        out_shape=[
            jax.ShapeDtypeStruct((rows, width), F32),
            jax.ShapeDtypeStruct((rows, width), F32),
            jax.ShapeDtypeStruct((rows, width), BF16),
            jax.ShapeDtypeStruct((ff, rows), BF16),
            jax.ShapeDtypeStruct((rows, ff), BF16),
            jax.ShapeDtypeStruct((width, rows), BF16),
            jax.ShapeDtypeStruct((width, rows), BF16),
            jax.ShapeDtypeStruct((8, width), F32),
            jax.ShapeDtypeStruct((1, ff), F32),
        ]
        + [jax.ShapeDtypeStruct((rows, own), BF16)] * parts,
        compiler_params=params(),
        cost_estimate=cost(8 * rows * width * ff, 4 * width * ff + 24 * rows * width),
        name="feed_forward",
    )(place, *context, hidden, cot, proj, vecs, fc1, fc1_bias, fc2)


def post_kernel(lead_ref, tail_ref, hidden_ref, d_middle_ref, gain_ref, w_ref, din_ref, dskip_ref, low_ref, vec_ref):
    width = hidden_ref.shape[1]
    upstream = jnp.concatenate([lead_ref[...].astype(F32), tail_ref[...].astype(F32)], 0)
    scaled, factor = normalize(hidden_ref[...])
    d_hidden = d_middle_ref[...] + norm_back(upstream, scaled, factor, gain_ref[...])
    low = d_hidden.astype(BF16)
    low_ref[...] = low
    vec_ref[0:1] = jnp.sum(d_hidden, axis=0, keepdims=True)
    vec_ref[1:2] = jnp.sum(upstream * scaled, axis=0, keepdims=True)
    vec_ref[2:3] = jnp.sum(upstream, axis=0, keepdims=True)
    vec_ref[3:] = jnp.zeros((5, width), F32)
    din_ref[...] = dot_nt(low, w_ref[:width])
    dskip_ref[...] = dot_nt(low, w_ref[width:])


def post(lead, tail, hidden, d_middle, gain, w):
    rows, width = hidden.shape
    return pl.pallas_call(
        post_kernel,
        out_shape=(
            jax.ShapeDtypeStruct((rows, width), F32),
            jax.ShapeDtypeStruct((rows, width), F32),
            jax.ShapeDtypeStruct((rows, width), BF16),
            jax.ShapeDtypeStruct((8, width), F32),
        ),
        compiler_params=params(),
        cost_estimate=cost(4 * rows * width * width, 4 * width * width + 20 * rows * width),
        name="input_back",
    )(lead, tail, hidden, d_middle, gain, w)


def pair_kernel(count, where_ref, *refs):
    out_ref = refs[4 * count]
    at = 0
    for index in range(count):
        own_t, peer_t, own, peer = refs[4 * index : 4 * index + 4]
        size = own_t.shape[2]
        out_ref[0, pl.ds(at, size)] = (
            dot(own_t[0, 0], own[...]) + dot(peer_t[0], peer[...])
        ).astype(BF16)
        at += size


def pair_grads(where, groups):
    depth = groups[0][0].shape[0]
    width = groups[0][2].shape[1]
    in_specs, operands, height, flops = [], [], 0, 0
    for own_t, peer_t, own, peer in groups:
        size, rows = own_t.shape[2:]
        in_specs += [
            pl.BlockSpec((1, 1, size, rows), lambda z, w: (z, w[0], 0, 0)),
            pl.BlockSpec((1, size, rows), lambda z, w: (z, 0, 0)),
            pl.BlockSpec((rows, width), lambda z, w: (0, 0)),
            pl.BlockSpec((rows, width), lambda z, w: (0, 0)),
        ]
        operands += [own_t, peer_t, own, peer]
        height += size
        flops += 4 * depth * size * rows * width
    return pl.pallas_call(
        functools.partial(pair_kernel, len(groups)),
        grid_spec=pltpu.PrefetchScalarGridSpec(
            num_scalar_prefetch=1,
            grid=(depth,),
            in_specs=in_specs,
            out_specs=pl.BlockSpec((1, height, width), lambda z, w: (z, 0, 0)),
        ),
        out_shape=jax.ShapeDtypeStruct((depth, height, width), BF16),
        compiler_params=params(),
        cost_estimate=cost(flops, 4 * depth * height * width),
        name="pair_grads",
    )(where, *operands)


def column_kernel(where_ref, own_t, peer_t, own, peer, out_ref):
    for z in range(own_t.shape[0]):
        out_ref[0, z] = (dot(own_t[z, 0], own[...]) + dot(peer_t[z], peer[...])).astype(BF16)


def column_grads(where, parts, own_t, peer_t, own, peer):
    depth, _, size, rows = own_t.shape
    width = own.shape[1] // parts
    return pl.pallas_call(
        column_kernel,
        grid_spec=pltpu.PrefetchScalarGridSpec(
            num_scalar_prefetch=1,
            grid=(parts,),
            in_specs=[
                pl.BlockSpec((depth, 1, size, rows), lambda k, w: (0, w[0], 0, 0)),
                pl.BlockSpec((depth, size, rows), lambda k, w: (0, 0, 0)),
                pl.BlockSpec((rows, width), lambda k, w: (0, k ^ w[1])),
                pl.BlockSpec((rows, width), lambda k, w: (0, k ^ w[1])),
            ],
            out_specs=pl.BlockSpec((1, depth, size, width), lambda k, w: (k, 0, 0, 0)),
        ),
        out_shape=jax.ShapeDtypeStruct((parts, depth, size, width), BF16),
        compiler_params=params(),
        cost_estimate=cost(
            4 * parts * depth * size * rows * width, 4 * parts * depth * size * width
        ),
        name="column_grads",
    )(where, own_t, peer_t, own, peer)


def heads_kernel(normed_ref, dt_ref, out_ref):
    out_ref[...] = lax.dot_general(
        normed_ref[...], dt_ref[...], (((0,), (1,)), ((), ())), preferred_element_type=F32
    ).astype(BF16)


def heads_grads(normed_all, d_triple_t):
    total, width = normed_all.shape
    wide = d_triple_t.shape[0]
    return pl.pallas_call(
        heads_kernel,
        out_shape=jax.ShapeDtypeStruct((width, wide), BF16),
        compiler_params=params(),
        cost_estimate=cost(2 * total * width * wide, 2 * total * (width + wide)),
        name="heads_grads",
    )(normed_all, d_triple_t)


def columns_kernel(place_ref, *refs):
    out_ref = refs[-1]
    size = refs[0].shape[1]
    for k in range(len(refs) - 1):
        at = pl.multiple_of((place_ref[0] ^ k) * size, LANES)
        out_ref[:, pl.ds(at, size)] = refs[k][...].astype(F32)


def put_columns(place, pieces):
    height, size = pieces[0].shape
    count = len(pieces)
    return pl.pallas_call(
        columns_kernel,
        in_specs=[pl.BlockSpec(memory_space=pltpu.SMEM)]
        + [pl.BlockSpec(memory_space=pltpu.VMEM)] * count,
        out_shape=jax.ShapeDtypeStruct((height, count * size), F32),
        compiler_params=params(),
        cost_estimate=cost(1e6, 6 * count * height * size),
        name="put_columns",
    )(place, *pieces)


def head_columns_kernel(place_ref, *refs):
    out_ref = refs[-1]
    count = len(refs) - 1
    size = refs[0].shape[1] // 3
    for j in range(count):
        value = refs[0][...]
        for k in range(1, count):
            value = jnp.where((place_ref[0] ^ k) == j, refs[k][...], value)
        value = value.astype(F32)
        for which in range(3):
            at = (which * count + j) * size
            out_ref[:, at : at + size] = value[:, which * size : (which + 1) * size]


def put_heads(place, pieces):
    height, size = pieces[0].shape
    count = len(pieces)
    return pl.pallas_call(
        head_columns_kernel,
        in_specs=[pl.BlockSpec(memory_space=pltpu.SMEM)]
        + [pl.BlockSpec(memory_space=pltpu.VMEM)] * count,
        out_shape=jax.ShapeDtypeStruct((height, count * size), F32),
        compiler_params=params(),
        cost_estimate=cost(1e6, 6 * count * height * size),
        name="put_heads",
    )(place, *pieces)


def across(value, size, bit):
    return lax.ppermute(value, "seq", [(i, i ^ bit) for i in range(size)])


def other_core(value, size):
    return lax.ppermute(value, "batch", [(i, i ^ 1) for i in range(size)])


def plus(*terms):
    total = terms[0].astype(F32)
    for term in terms[1:]:
        total = total + term.astype(F32)
    return total.astype(BF16)


def bits_of(size):
    return [1 << i for i in range(size.bit_length() - 1)]


def everywhere(value, size):
    if size != 4:
        return [value] + [across(value, size, k) for k in range(1, size)]
    half = value.shape[0] // 2
    near, far = across(value, size, 1), across(value, size, 2)
    lead, tail = across(near[:half], size, 2), across(far[half:], size, 1)
    return [value, near, far, jnp.concatenate([lead, tail], 0)]


def scattered(value, size, bits):
    left = list(range(size))
    for bit in bits:
        keep = [i for i, k in enumerate(left) if not k & bit]
        send = [i for i, k in enumerate(left) if k & bit]
        pick = lambda which: jnp.concatenate([value[i : i + 1] for i in which], 0)
        value = plus(pick(keep), across(pick(send), size, bit))
        left = [left[i] for i in keep]
    return value[0]


def summed(value, size):
    half = (value.shape[0] // 2 + 7) // 8 * 8
    bits = bits_of(size)
    done = []
    for piece, order in ((value[:half], bits), (value[half:], bits[::-1])):
        for bit in order:
            piece = plus(piece, across(piece, size, bit))
        done.append(piece)
    return jnp.concatenate(done, 0)


def down_the_line(value, size, at):
    depth = value.shape[0]
    pick = lambda index: lax.dynamic_index_in_dim(
        value, jnp.clip(index, 0, depth - 1), 0, keepdims=False
    )
    up = down = None
    for t in range(depth - 1):
        send_up = pick(depth - 1 - t + at)
        send_down = pick(t - (depth - 1 - at))
        if t:
            send_up, send_down = plus(send_up, up), plus(send_down, down)
        up = lax.ppermute(
            send_up,
            "batch",
            [(2 * z + c, 2 * z + 2 + c) for z in range(depth - 1) if z <= t for c in (0, 1)],
        )
        down = lax.ppermute(
            send_down,
            "batch",
            [
                (2 * z + c, 2 * z - 2 + c)
                for z in range(1, depth)
                if z >= depth - 1 - t
                for c in (0, 1)
            ],
        )
    return plus(pick(at), up, down)


MESH = pl.DeviceIdType.MESH


def flip(value, k):
    if k == 0:
        return value
    if k == 1:
        return value + 1 - 2 * (value % 2)
    if k == 2:
        return value + 2 - 4 * (value // 2)
    return 3 - value


def add_rows(into, other):
    if len(into.shape) > 2:
        for i in range(into.shape[0]):
            add_rows(into.at[i], other.at[i])
        return
    tile = 16

    def body(i, carry):
        at = pl.ds(pl.multiple_of(i * tile, tile), tile)
        into[at] = (into[at].astype(F32) + other[at].astype(F32)).astype(BF16)
        return carry

    lax.fori_loop(0, into.shape[0] // tile, body, 0)


class Wires:
    def __init__(self, send_sems, recv_sems):
        self.send_sems, self.recv_sems, self.made = send_sems, recv_sems, []

    def copy(self, src, dst, device, when=None):
        index = len(self.made)
        made = Wire(
            pltpu.make_async_remote_copy(
                src_ref=src,
                dst_ref=dst,
                send_sem=self.send_sems.at[index],
                recv_sem=self.recv_sems.at[index],
                device_id=device,
                device_id_type=MESH,
            ),
            when,
        )
        self.made.append(made)
        return made

    def drain(self):
        for wire in self.made:
            if wire.when is None:
                wire.copy.wait_send()
            else:
                pl.when(wire.when)(wire.copy.wait_send)


class Wire:
    def __init__(self, copy, when):
        self.copy, self.when = copy, when
        self.start, self.arrive = copy.start, copy.wait_recv


class Line:
    def __init__(self, wires, depth, chip, up_to, down_to, own, up_in, down_in, begun=False):
        self.depth, self.chip, self.own, self.begun = depth, chip, own, begun
        self.up_in, self.down_in = up_in, down_in
        last = depth - 1
        self.up = {
            d: wires.copy(
                own(d),
                up_in.at[d - 1],
                up_to,
                (chip < d) & (chip > 0) if begun and d == last else chip < d,
            )
            for d in range(1, depth)
        }
        self.down = {
            d: wires.copy(
                own(d),
                down_in.at[d],
                down_to,
                (chip > d) & (chip < last) if begun and d == 0 else chip > d,
            )
            for d in range(last)
        }

    def hop(self, t):
        last = self.depth - 1
        for d in range(1, self.depth):
            z = d - (last - t)
            if 0 <= z < d:

                @pl.when(self.chip == z)
                def _():
                    if z > 0 and not (self.begun and t == 1):
                        self.up[d].arrive()
                        add_rows(self.own(d), self.up_in.at[d - 1])
                    self.up[d].start()

                @pl.when(self.chip == last - z)
                def _():
                    if z > 0 and not (self.begun and t == 1):
                        self.down[last - d].arrive()
                        add_rows(self.own(last - d), self.down_in.at[last - d])
                    self.down[last - d].start()

    def finish(self):
        for d in range(self.depth):

            @pl.when(self.chip == d)
            def _():
                if d > 0:
                    self.up[d].arrive()
                    add_rows(self.own(d), self.up_in.at[d - 1])
                if d < self.depth - 1:
                    self.down[d].arrive()
                    add_rows(self.own(d), self.down_in.at[d])


class Square:
    def __init__(self, wires, to, own, in_one, in_two, src=None, begun=False):
        self.own, self.in_one, self.in_two = own, in_one, in_two
        src = src or own
        self.one, self.two = [], []
        for h, (f, g) in enumerate(((1, 2), (2, 1))):
            if not begun:
                self.one.append(
                    (
                        wires.copy(src(h, 3), in_one.at[h, 1], to[f]),
                        wires.copy(src(h, f), in_one.at[h, 0], to[f]),
                    )
                )
        for h, (f, g) in enumerate(((1, 2), (2, 1))):
            self.two.append(wires.copy(own(h, g), in_two.at[h], to[g]))

    def start(self):
        for i in range(2):
            for h in range(2):
                self.one[h][i].start()

    def middle(self):
        for h, g in ((0, 2), (1, 1)):
            self.one[h][0].arrive()
            add_rows(self.own(h, g), self.in_one.at[h, 1])
            self.two[h].start()
        for h in range(2):
            self.one[h][1].arrive()
            add_rows(self.own(h, 0), self.in_one.at[h, 0])

    def finish(self):
        for h in range(2):
            self.two[h].arrive()
            add_rows(self.own(h, 0), self.in_two.at[h])


class Spread:
    def __init__(self, wires, to, slots):
        rows = slots.shape[1]
        cut = (rows // 2 + 15) // 16 * 16
        self.near = wires.copy(slots.at[0], slots.at[1], to[1])
        self.far = wires.copy(slots.at[0], slots.at[2], to[2])
        lead, tail = pl.ds(0, cut), pl.ds(cut, rows - cut)
        self.lead = wires.copy(slots.at[1, lead], slots.at[3, lead], to[2])
        self.tail = wires.copy(slots.at[2, tail], slots.at[3, tail], to[1])

    def start(self):
        self.near.start()
        self.far.start()

    def relay(self):
        self.near.arrive()
        self.lead.start()
        self.far.arrive()
        self.tail.start()

    def finish(self):
        self.lead.arrive()
        self.tail.arrive()


def reduce_kernel(
    late_hbm,
    up_hbm,
    down_hbm,
    first_a_hbm,
    first_b_hbm,
    lead_hbm,
    tail_hbm,
    normed_hbm,
    dt_hbm,
    joined_hbm,
    joined_peer_hbm,
    hidden_hbm,
    d_middle_hbm,
    w_hbm,
    gain_ref,
    vec_two_ref,
    fc1_bias_ref,
    g_late_hbm,
    g_first_hbm,
    g_heads_hbm,
    g_skip_hbm,
    din_hbm,
    dskip_hbm,
    cond_ref,
    vec_ref,
    l_own,
    l_up,
    l_down,
    f_own,
    f_in,
    f_up,
    f_down,
    f_all,
    q_own,
    q_sum,
    q_up,
    q_down,
    q_all,
    s_own,
    s_one,
    s_two,
    s_z,
    s_up,
    s_down,
    s_all,
    d_own,
    d_one,
    d_two,
    p_one,
    p_two,
    p_all,
    low_ref,
    low_peer,
    c_all,
    v_own,
    v_in,
    send_sems,
    recv_sems,
    local_sems,
):
    depth, late_rows, width = late_hbm.shape
    rows = hidden_hbm.shape[0]
    half = rows // 2
    mid = depth // 2
    slots = c_all.shape[1]
    place = lax.axis_index("seq")
    index = lax.axis_index("batch")
    chip, core = index // 2, index % 2
    last = depth - 1
    to = {1: (index, flip(place, 1)), 2: (index, flip(place, 2)), 3: (index, flip(place, 3))}
    other = (index + 1 - 2 * core, place)
    up_to, down_to = (index + 2, place), (index - 2, place)

    barrier = pltpu.get_barrier_semaphore()
    for device in (to[1], to[2], to[3], other):
        pl.semaphore_signal(barrier, inc=1, device_id=device, device_id_type=MESH)

    @pl.when(chip < last)
    def _():
        pl.semaphore_signal(barrier, inc=1, device_id=up_to, device_id_type=MESH)

    @pl.when(chip > 0)
    def _():
        pl.semaphore_signal(barrier, inc=1, device_id=down_to, device_id_type=MESH)

    pl.semaphore_wait(barrier, 4 + jnp.minimum(chip, 1) + jnp.minimum(last - chip, 1))

    wires = Wires(send_sems, recv_sems)
    taken = [0]

    def local(src, dst):
        taken[0] += 1
        copy = pltpu.make_async_copy(src, dst, local_sems.at[taken[0] - 1])
        copy.start()
        return copy

    d_hbm = (lead_hbm, tail_hbm)
    norm_sum = Square(
        wires,
        to,
        lambda h, k: d_own.at[h, (0, 1, 1, None)[k]],
        d_one,
        d_two,
        src=lambda h, k: d_hbm[h].at[k],
    )
    norm_sum.start()
    d_loads = [
        local(d_hbm[h].at[k], d_own.at[h, i]) for h, ks in ((0, (0, 2)), (1, (0, 1))) for i, k in enumerate(ks)
    ]
    l_loads = [local(late_hbm.at[z], l_own.at[z, pl.ds(0, late_rows)]) for z in range(depth)]
    f_loads = [local(first_a_hbm, f_own.at[0]), local(first_b_hbm, f_own.at[1])]

    l_line = Line(
        wires,
        depth,
        chip,
        up_to,
        down_to,
        lambda d: l_own.at[d, pl.ds(0, late_rows)],
        l_up,
        l_down,
        begun=True,
    )
    for copy in l_loads:
        copy.wait()
    l_own[:, late_rows:] = jnp.zeros((depth, l_own.shape[1] - late_rows, width), BF16)
    up_sem, down_sem = local_sems.at[taken[0]], local_sems.at[taken[0] + 1]
    taken[0] += 2

    @pl.when(chip == 1)
    def _():
        copy = pltpu.make_async_copy(up_hbm, l_up.at[last - 1], up_sem)
        copy.start()
        copy.wait()
        add_rows(l_own.at[last, pl.ds(0, late_rows)], l_up.at[last - 1])

    @pl.when(chip == last - 1)
    def _():
        copy = pltpu.make_async_copy(down_hbm, l_down.at[0], down_sem)
        copy.start()
        copy.wait()
        add_rows(l_own.at[0, pl.ds(0, late_rows)], l_down.at[0])

    l_line.hop(1)

    def heads_part(normed, dt):
        loads = [local(normed_hbm, normed), local(dt_hbm, dt)]
        for copy in loads:
            copy.wait()
        height = normed.shape[1] // (2 * depth)
        step = 3 * LANES
        for part in range(normed.shape[1] // step):
            grads = lax.dot_general(
                normed[:, part * step : (part + 1) * step],
                dt[...],
                (((0,), (1,)), ((), ())),
                preferred_element_type=F32,
            ).astype(BF16)
            q_own[pl.ds(part * step, step)] = grads

    pl.run_scoped(
        heads_part, pltpu.VMEM(normed_hbm.shape, BF16), pltpu.VMEM(dt_hbm.shape, BF16)
    )
    height = q_sum.shape[1]
    q_swap = [
        wires.copy(
            q_own.at[pl.ds(pl.multiple_of((2 * z + 1 - core) * height, 16), height)],
            q_sum.at[z],
            other,
        )
        for z in range(depth)
    ]
    for wire in q_swap:
        wire.start()

    for copy in d_loads:
        copy.wait()
    norm_sum.middle()

    for copy in f_loads:
        copy.wait()
    f_two = [
        wires.copy(f_own.at[h, 1], f_in.at[h], to[2 - h]) for h in range(2)
    ]
    for wire in f_two:
        wire.start()
    for z, wire in enumerate(q_swap):
        wire.arrive()
        add_rows(q_sum.at[z], q_own.at[pl.ds(pl.multiple_of((2 * z + core) * height, 16), height)])
    q_line = Line(wires, depth, chip, up_to, down_to, lambda d: q_sum.at[d], q_up, q_down)
    q_line.hop(0)

    norm_sum.finish()
    low_swap = wires.copy(low_ref, low_peer, other)
    v_swap = wires.copy(v_own.at[0], v_in.at[0], other)

    def back_part(hidden, d_middle):
        loads = [local(hidden_hbm, hidden), local(d_middle_hbm, d_middle)]
        for copy in loads:
            copy.wait()
        upstream = jnp.concatenate(
            [d_own[0, 0].astype(F32), d_own[1, 0].astype(F32)], 0
        )
        scaled, factor = normalize(hidden[...])
        d_hidden = d_middle[...] + norm_back(upstream, scaled, factor, gain_ref[...])
        low_ref[...] = d_hidden.astype(BF16)
        low_swap.start()
        v_own[0] = jnp.zeros(v_own.shape[1:], F32)
        v_own[0, 0:1] = jnp.sum(d_hidden, axis=0, keepdims=True)
        v_own[0, 1:2] = jnp.sum(upstream * scaled, axis=0, keepdims=True)
        v_own[0, 2:3] = jnp.sum(upstream, axis=0, keepdims=True)
        v_own[0, 3:7] = vec_two_ref[0:4]
        v_own[0, 8:12] = fc1_bias_ref[...]
        v_swap.start()

    pl.run_scoped(back_part, pltpu.VMEM(hidden_hbm.shape, F32), pltpu.VMEM(hidden_hbm.shape, F32))

    low_swap.arrive()

    def skip_part(joined, peer):
        loads = [local(joined_hbm.at[:, core], joined), local(joined_peer_hbm, peer)]
        for copy in loads:
            copy.wait()
        chunk = joined.shape[1] // 4
        for z in range(depth):
            grads = dot(joined[z], low_ref[...]) + dot(peer[z], low_peer[...])
            for j in range(4):
                piece = grads[j * chunk : (j + 1) * chunk]
                piece = jnp.concatenate(
                    [piece, jnp.zeros((s_own.shape[2] - chunk, width), F32)], 0
                )
                s_own[flip(place, j), z] = piece.astype(BF16)

    pl.run_scoped(
        skip_part,
        pltpu.VMEM(joined_peer_hbm.shape, BF16),
        pltpu.VMEM(joined_peer_hbm.shape, BF16),
    )
    s_sum = Square(
        wires, to, lambda h, k: s_own.at[k, pl.ds(h * mid, mid)], s_one, s_two
    )
    s_sum.start()

    c_go = [wires.copy(c_all.at[0], c_all.at[k], to[k]) for k in (1, 2, 3)]

    def rows_part(w, stage):
        copy = local(w_hbm.at[pl.ds(0, width)], w)
        copy.wait()
        stage[...] = dot_nt(low_ref[...], w[...])
        c_all[0, :, :width] = stage[:slots].astype(BF16)
        copy = local(w_hbm.at[pl.ds(width, width)], w)
        out = local(stage, din_hbm)
        copy.wait()
        out.wait()
        stage[...] = dot_nt(low_ref[...], w[...])
        c_all[0, :, width:] = stage[:slots].astype(BF16)
        for wire in c_go:
            wire.start()
        local(stage, dskip_hbm).wait()

    pl.run_scoped(rows_part, pltpu.VMEM((width, width), BF16), pltpu.VMEM((rows, width), F32))

    v_swap.arrive()
    v_own[1] = v_own[0] + v_in[0]
    v_up = wires.copy(v_own.at[2], v_in.at[1], up_to, chip < last)
    v_down = wires.copy(v_own.at[3], v_in.at[2], down_to, chip > 0)

    for h in range(2):
        f_two[h].arrive()
        add_rows(f_own.at[h, 0], f_in.at[h])
    f_line = Line(
        wires,
        depth,
        chip,
        up_to,
        down_to,
        lambda d: f_own.at[d // mid, 0, d % mid],
        f_up,
        f_down,
    )
    f_line.hop(0)
    l_line.hop(2)
    q_line.hop(1)
    s_sum.middle()
    f_line.hop(1)
    for t in range(3, last):
        l_line.hop(t)
    for t in range(2, last):
        q_line.hop(t)
    s_sum.finish()
    for d in range(depth):
        s_z[d] = s_own[0, d]
    s_line = Line(wires, depth, chip, up_to, down_to, lambda d: s_z.at[d], s_up, s_down)
    s_line.hop(0)
    for t in range(2, last):
        f_line.hop(t)
    q_line.finish()
    q_all[0] = q_sum[chip]
    q_go = Spread(wires, to, q_all)
    q_go.start()

    v_own[2] = v_own[1]
    v_own[3] = v_own[1]

    @pl.when(chip > 0)
    def _():
        v_up.arrive()
        v_own[2] = v_own[1] + v_in[1]

    @pl.when(chip < last)
    def _():
        v_up.start()

    @pl.when(chip < last)
    def _():
        v_down.arrive()
        v_own[3] = v_own[1] + v_in[2]

    @pl.when(chip > 0)
    def _():
        v_down.start()

    v_own[4] = v_own[2] + v_own[3] - v_own[1]
    v_near = wires.copy(v_own.at[4], v_in.at[3], to[1])
    v_near.start()
    s_line.hop(1)

    l_line.finish()
    chunk = p_all.shape[1]
    part = chunk // 2

    def p_rows(h, k):
        at = pl.multiple_of(flip(place, k) * chunk + h * part, 16)
        return l_own.at[chip, pl.ds(at, part)]

    p_sum = Square(wires, to, p_rows, p_one, p_two)
    p_sum.start()
    f_line.finish()
    f_all[0] = f_own[chip // mid, 0, chip % mid]
    f_go = Spread(wires, to, f_all)
    q_go.relay()
    f_go.start()
    for t in range(2, last):
        s_line.hop(t)
    p_sum.middle()
    v_near.arrive()
    v_own[5] = v_own[4] + v_in[3]
    v_far = wires.copy(v_own.at[5], v_in.at[4], to[2])
    v_far.start()
    s_line.finish()
    s_all[0] = s_z[chip]
    s_go = Spread(wires, to, s_all)
    s_go.start()
    p_sum.finish()
    p_all[0, pl.ds(0, part)] = p_rows(0, 0)[...]
    p_all[0, pl.ds(part, part)] = p_rows(1, 0)[...]
    p_go = Spread(wires, to, p_all)
    p_go.start()
    f_go.relay()
    q_go.finish()

    def heads_out(stage):
        size = q_all.shape[2] // 3
        for j in range(4):
            value = q_all[flip(place, j)].astype(F32)
            for which in range(3):
                at = (which * 4 + j) * size
                stage[:, at : at + size] = value[:, which * size : (which + 1) * size]
        local(stage, g_heads_hbm).wait()

    pl.run_scoped(heads_out, pltpu.VMEM(g_heads_hbm.shape, F32))
    for wire in c_go:
        wire.arrive()
    for j in range(4):
        cond_ref[j * slots : (j + 1) * slots] = c_all[flip(place, j)].astype(F32)
    v_far.arrive()
    vec_ref[...] = v_own[5] + v_in[4]
    s_go.relay()
    p_go.relay()
    f_go.finish()

    def first_out(stage):
        for j in range(4):
            stage[:, j * width : (j + 1) * width] = f_all[flip(place, j)].astype(F32)
        local(stage, g_first_hbm).wait()

    pl.run_scoped(first_out, pltpu.VMEM(g_first_hbm.shape, F32))
    s_go.finish()

    def skip_out(stage):
        size = stage.shape[0] // 4
        for j in range(4):
            stage[j * size : (j + 1) * size] = s_all[flip(place, j), :size].astype(F32)
        local(stage, g_skip_hbm).wait()

    pl.run_scoped(skip_out, pltpu.VMEM(g_skip_hbm.shape, F32))
    p_go.finish()

    def late_out(stage):
        for j in range(4):
            stage[j * chunk : (j + 1) * chunk] = p_all[flip(place, j)].astype(F32)
        local(stage.at[pl.ds(0, late_rows)], g_late_hbm).wait()

    pl.run_scoped(late_out, pltpu.VMEM((4 * chunk, width), F32))
    wires.drain()


def reduce_all(
    late, up, down, first_a, first_b, lead, tail, normed_all, d_triple_t, joined, joined_peer,
    hidden, d_middle, w, gain, vec_two, fc1_bias_grad, slots,
):
    depth, late_rows, width = late.shape
    rows = hidden.shape[0]
    mid = depth // 2
    batch = 2 * depth
    small = first_a.shape[2]
    own = d_triple_t.shape[0]
    chunk = (-(-late_rows // 4) + 31) // 32 * 32
    skip_chunk = (joined.shape[2] // 4 + 15) // 16 * 16
    half = rows // 2
    v = lambda *shape: pltpu.VMEM(shape, BF16)
    ends = depth - 1
    scratch = [
        v(depth, 4 * chunk, width), v(ends, late_rows, width), v(ends, late_rows, width),
        v(2, 2, mid, small, width), v(2, mid, small, width), v(ends, small, width), v(ends, small, width),
        v(4, small, width),
        v(width, own), v(depth, small, own), v(ends, small, own), v(ends, small, own), v(4, small, own),
        v(4, depth, skip_chunk, width), v(2, 2, mid, skip_chunk, width), v(2, mid, skip_chunk, width),
        v(depth, skip_chunk, width), v(ends, skip_chunk, width), v(ends, skip_chunk, width),
        v(4, skip_chunk, width),
        v(2, 2, half, width), v(2, 2, half, width), v(2, half, width),
        v(2, 2, chunk // 2, width), v(2, chunk // 2, width), v(4, chunk, width),
        v(rows, width), v(rows, width), v(4, slots, 2 * width),
        pltpu.VMEM((6, 16, width), F32), pltpu.VMEM((5, 16, width), F32),
        pltpu.SemaphoreType.DMA((96,)), pltpu.SemaphoreType.DMA((96,)), pltpu.SemaphoreType.DMA((64,)),
    ]
    hbm = pl.BlockSpec(memory_space=pl.ANY)
    vmem = pl.BlockSpec(memory_space=pltpu.VMEM)
    f = lambda *shape: jax.ShapeDtypeStruct(shape, F32)
    return pl.pallas_call(
        reduce_kernel,
        in_specs=[hbm] * 14 + [vmem] * 3,
        out_specs=[hbm] * 6 + [vmem] * 2,
        out_shape=[
            f(late_rows, width),
            f(small, 4 * width),
            f(small, 4 * own),
            f(joined.shape[2], width),
            f(rows, width),
            f(rows, width),
            f(4 * slots, 2 * width),
            f(16, width),
        ],
        scratch_shapes=scratch,
        compiler_params=pltpu.CompilerParams(
            vmem_limit_bytes=VMEM_LIMIT, collective_id=0, has_side_effects=True
        ),
        cost_estimate=cost(1e10, 1e8),
        name="reduce_all",
    )(
        late, up, down, first_a, first_b, lead, tail, normed_all, d_triple_t, joined, joined_peer,
        hidden, d_middle, w, gain, vec_two, fc1_bias_grad.reshape(-1, width),
    )


def per_device(
    batch,
    parts,
    image_in,
    cond_in,
    skip_image,
    skip_cond,
    caption_len,
    skip_weight,
    skip_bias,
    first_gain,
    first_bias,
    qkv_weight,
    proj_weight,
    proj_bias,
    second_gain,
    second_bias,
    fc1_weight,
    fc1_bias,
    fc2_weight,
    fc2_bias,
    grad_image,
    grad_cond,
):
    conds = cond_in.shape[0]
    width = image_in.shape[2]
    images = image_in.shape[0]
    ff = fc1_weight.shape[1]
    slots = SLOTS // parts
    rows = slots + images
    total = rows * parts
    heads = HEADS // parts
    depth = batch // 2
    place = lax.axis_index("seq")
    index = lax.axis_index("batch")
    core, chip = index % 2, index // 2
    where = jnp.stack([core, place]).astype(jnp.int32)

    def own_rows(cond, image):
        padded = jnp.pad(cond[:, 0], ((0, SLOTS - conds), (0, 0)))
        lead = lax.dynamic_slice_in_dim(padded, place * slots, slots, 0)
        return jnp.concatenate([lead, image[:, 0]], 0)

    x = own_rows(cond_in, image_in)
    s = own_rows(skip_cond, skip_image)
    cot = own_rows(grad_cond, grad_image)

    hidden, normed, joined_t = pre(
        x, s, skip_weight, skip_bias[None], first_gain[None], first_bias[None]
    )
    normed_all = jnp.concatenate(everywhere(normed, parts), 0)
    own = heads * HEAD_DIM
    w_heads = heads_weight(where[1:], qkv_weight, heads)
    order = place ^ jnp.arange(parts, dtype=jnp.int32)
    position = order[:, None] * slots + jnp.arange(rows, dtype=jnp.int32)[None]
    valid = (jnp.arange(rows)[None] >= slots) | (position <= caption_len[0])
    kbias = jnp.where(
        (jnp.arange(LANES) == HEAD_DIM)[None] & ~valid.reshape(total, 1), F32(-1e30), F32(0)
    )
    qkv, lse, *ctx_parts = attend(parts, normed_all, w_heads, kbias)
    context = [ctx_parts[0]] + [across(ctx_parts[k], parts, k) for k in range(1, parts)]

    zero = jnp.zeros_like(proj_bias)
    vecs = jnp.stack([proj_bias, second_gain, second_bias, fc2_bias, zero, zero, zero, zero])
    (
        out,
        d_middle,
        d_branch,
        active_t,
        d_pre,
        normed2_t,
        ctx_t,
        vec_two,
        fc1_bias_grad,
        *d_ctx_parts,
    ) = mlp(
        parts,
        where[1:],
        context,
        hidden,
        cot,
        proj_weight,
        vecs,
        fc1_weight,
        fc1_bias[None],
        fc2_weight,
    )
    d_context = [d_ctx_parts[0]] + [across(d_ctx_parts[k], parts, k) for k in range(1, parts)]

    def by_core(turned_rows):
        blocks = turned_rows.reshape(depth, 2, -1, rows)
        send = lax.dynamic_index_in_dim(blocks, 1 - core, 1, keepdims=False)
        return blocks, other_core(send, batch)

    active_b, active_p = by_core(active_t)
    normed2_b, normed2_p = by_core(normed2_t)
    ctx_b, ctx_p = by_core(ctx_t)
    joined_b, joined_p = by_core(joined_t)
    cot_p, d_pre_p, d_branch_p = (other_core(v, batch) for v in (cot, d_pre, d_branch))
    late = pair_grads(
        where, [(active_b, active_p, cot, cot_p), (ctx_b, ctx_p, d_branch, d_branch_p)]
    )
    by_columns = (ff // parts) % LANES == 0
    fast = parts == 4 and depth == 4 and by_columns
    if by_columns:
        first = column_grads(where, parts, normed2_b, normed2_p, d_pre, d_pre_p)
        late, first, d_context = lax.optimization_barrier((late, first, d_context))
        middle = depth // 2
    if fast:
        up = lax.ppermute(late[-1], "batch", [(c, 2 + c) for c in (0, 1)])
        down = lax.ppermute(late[0], "batch", [(batch - 2 + c, batch - 4 + c) for c in (0, 1)])
        first_a = (first[0::2, :middle], across(first[1::2, :middle], parts, 1))
        first_b = (first[:2, middle:], across(first[2:, middle:], parts, 2))
    elif by_columns:
        first = jnp.concatenate(
            [
                scattered(first[:, :middle], parts, bits_of(parts)),
                scattered(first[:, middle:], parts, bits_of(parts)[::-1]),
            ],
            0,
        )
    if not by_columns:
        first = pair_grads(where, [(normed2_b, normed2_p, d_pre, d_pre_p)])
    def all_conds(lead):
        pieces = [lead] + [across(lead, parts, k) for k in range(1, parts)]
        full = jnp.zeros((SLOTS, lead.shape[1]), F32)
        for k in range(parts):
            full = lax.dynamic_update_slice_in_dim(
                full, pieces[k].astype(F32), (place ^ k) * slots, 0
            )
        return full[:conds, None]

    d_triple_t, d_lead, d_tail = attend_back(parts, d_context, qkv, lse, w_heads)
    if fast:
        d_lead, d_tail, d_triple_t, up, down, first_a, first_b = lax.optimization_barrier(
            (d_lead, d_tail, d_triple_t, up, down, first_a, first_b)
        )
        g_late, wgrad_fc1, wgrad_qkv, wgrad_skip, d_in, d_skip, d_cond, vec = reduce_all(
            late, up, down, plus(*first_a), plus(*first_b), d_lead, d_tail, normed_all,
            d_triple_t, joined_b, joined_p, hidden, d_middle, skip_weight, first_gain[None],
            vec_two, fc1_bias_grad, slots,
        )
        fc2_rows = ff // batch
        share = lambda v: lax.dynamic_slice_in_dim(v, index * (v.size // batch), v.size // batch, 0)
        vec = [share(vec[i]) for i in (0, 1, 2, 5, 3, 4)] + [share(vec[8:12].reshape(-1)), share(vec[6])]
        return (
            out[slots:, None],
            all_conds(out[:slots].astype(BF16)),
            d_in[slots:, None],
            d_cond[:conds, None, :width],
            d_skip[slots:, None],
            d_cond[:conds, None, width:],
            wgrad_skip,
            vec[0],
            vec[1],
            vec[2],
            wgrad_qkv,
            g_late[fc2_rows:],
            vec[3],
            vec[4],
            vec[5],
            wgrad_fc1,
            vec[6],
            g_late[:fc2_rows],
            vec[7],
        )

    d_lead = scattered(d_lead, parts, bits_of(parts))
    d_tail = scattered(d_tail, parts, bits_of(parts)[::-1])
    heads_grad = heads_grads(normed_all, d_triple_t).reshape(depth, 2, -1, 3 * own)
    heads_grad = plus(
        lax.dynamic_index_in_dim(heads_grad, core, 1, keepdims=False),
        other_core(lax.dynamic_index_in_dim(heads_grad, 1 - core, 1, keepdims=False), batch),
    )
    heads_grad = everywhere(down_the_line(heads_grad, batch, chip), parts)
    wgrad_qkv = put_heads(where[1:], heads_grad)

    d_in, d_skip, d_low, vec_one = post(
        d_lead, d_tail, hidden, d_middle, first_gain[None], skip_weight
    )
    d_low_p = other_core(d_low, batch)
    last = pair_grads(where, [(joined_b, joined_p, d_low, d_low_p)])

    late = down_the_line(late, batch, chip)
    first = down_the_line(first, batch, chip)
    late = summed(late, parts)
    if by_columns:
        fc1_cols = everywhere(first, parts)
        wgrad_fc1 = put_columns(where[1:], fc1_cols)
    else:
        wgrad_fc1 = summed(first, parts).astype(F32)

    vectors = [
        vec_one[0],
        vec_one[1],
        vec_one[2],
        vec_two[2],
        vec_two[0],
        vec_two[1],
        fc1_bias_grad[0],
        vec_two[3],
    ]
    sizes = [v.shape[0] // batch for v in vectors]
    packed = jnp.concatenate([v.reshape(batch, -1) for v in vectors], 1)
    packed = packed.reshape(depth, 2, -1)
    packed = lax.dynamic_index_in_dim(packed, core, 1, keepdims=False) + other_core(
        lax.dynamic_index_in_dim(packed, 1 - core, 1, keepdims=False), batch
    )
    packed = jnp.pad(packed, ((0, 0), (0, 16 * width - packed.shape[1]))).reshape(depth, 16, width)
    last = jnp.concatenate([last, packed.astype(BF16)], 1)
    last = summed(down_the_line(last, batch, chip), parts)
    skip_rows = 2 * width // batch
    wgrad_skip = last[:skip_rows].astype(F32)
    flat = last[skip_rows:].reshape(-1).astype(F32)
    vector_out, at = [], 0
    for size in sizes:
        vector_out.append(flat[at : at + size])
        at += size
    fc2_rows = ff // batch
    wgrad_fc2 = late[:fc2_rows].astype(F32)
    wgrad_proj = late[fc2_rows:].astype(F32)

    out_cond = all_conds(out[:slots].astype(BF16))
    d_cond = all_conds(jnp.concatenate([d_in[:slots], d_skip[:slots]], 1).astype(BF16))
    return (
        out[slots:, None],
        out_cond,
        d_in[slots:, None],
        d_cond[:, :, :width],
        d_skip[slots:, None],
        d_cond[:, :, width:],
        wgrad_skip,
        vector_out[0],
        vector_out[1],
        vector_out[2],
        wgrad_qkv,
        wgrad_proj,
        vector_out[3],
        vector_out[4],
        vector_out[5],
        wgrad_fc1,
        vector_out[6],
        wgrad_fc2,
        vector_out[7],
    )


def solution(mesh):
    tokens, conds, shared = P("seq", "batch", None), P(None, "batch", None), P()
    return jax.shard_map(
        functools.partial(per_device, mesh.shape["batch"], mesh.shape["seq"]),
        mesh=mesh,
        in_specs=(tokens, conds, tokens, conds, P("batch")) + (shared,) * 13 + (tokens, conds),
        out_specs=(tokens, conds) * 3
        + (
            P("batch", None),
            P("batch"),
            P("batch"),
            P("batch"),
            P("batch", None),
            P("batch", None),
            P("batch"),
            P("batch"),
            P("batch"),
            P("batch", None),
            P("batch"),
            P("batch", None),
            P("batch"),
        ),
        check_vma=False,
    )
```

time: 1040 us -> 446 us (0.43)
  waiting for transfers between devices: 612 us -> 13.5 us
  Pallas kernels: 0 us -> 329 us
  matrix products: 213 us -> 0 us
  blocking collectives: 79.4 us -> 0 us
  other arithmetic: 44.5 us -> 11.3 us
  starting transfers between devices: 1.41 us -> 26.9 us
  between operations: 16.9 us -> 2.26 us
  local copies, waits for them, and re-layouts: 67.8 us -> 54.4 us
    reduce_scatter x6 -> x0, waiting for transfers between devices: 373 us -> none  [the longest x5 359 us: per_device(): lax.psum_scatter(shortened(rest_grads + mlp_grads), 'batch', scatter_dime...]
    pallas_call x0 -> x8, Pallas kernels: none -> 329 us  [the longest x1 191 us: reduce_all(): pl.pallas_call(reduce_kernel, in_specs=[hbm] * 14 + [vmem] * 3, out_specs...]
    dot_general x22 -> x0, matrix products: 185 us -> none  [the longest x5 43.5 us: times_transpose(): lax.dot_general(left, right, (((1,), (1,)), ((), ())), preferred_element_...]
    unnamed x20 -> x0, waiting for transfers between devices: 116 us -> none
    all_gather x3 -> x0, waiting for transfers between devices: 75.6 us -> none  [the longest x1 52.8 us: per_device(): lax.all_gather(local_pairs[cond_rows:], 'seq', axis=0, tiled=True)]
    psum x1 -> x0, waiting for transfers between devices: 47.7 us -> none  [per_device(): lax.psum(cond_vals.astype(jnp.bfloat16), 'seq').astype(jnp.float32)]
    all_gather x3 -> x0, blocking collectives: 36.3 us -> none  [the longest x1 13.7 us: per_device(): lax.all_gather(column_parts[1].astype(jnp.bfloat16), 'seq', axis=1, tiled...]
    sub x1 -> x0, matrix products: 28.6 us -> none  [per_device(): d_probs - row_delta]
  transfers between devices with their start and end apart: 15 -> 24, of which waited for: 13 -> 6; matrix products, arithmetic and copies ran while one was open for 13% -> 8% of each run, Pallas kernels for 0% -> 30%
where the time goes in v1:
time: 446 us; the launch traced here: 438 us
  Pallas kernels  329 us (74%)
  local copies, waits for them, and re-layouts  54.4 us (12%)
  starting transfers between devices  26.9 us (6%)
  waiting for transfers between devices  13.5 us (3%)
  other arithmetic  11.3 us (3%)
    pallas_call x1, Pallas kernels, reduce_all(): pl.pallas_call(reduce_kernel, in_specs=[hbm] * 14 + [vmem] * 3, out_specs...  191 us
    pallas_call x1, Pallas kernels, attend_back(): pl.pallas_call(functools.partial(attend_back_kernel, parts), grid=(heads,...  38.9 us
    pallas_call x1, Pallas kernels, mlp(): pl.pallas_call(functools.partial(mlp_kernel, parts), grid_spec=pltpu.Pref...  30.1 us
    pallas_call x1, Pallas kernels, pair_grads(): pl.pallas_call(functools.partial(pair_kernel, len(groups)), grid_spec=plt...  23.3 us
    pallas_call x1, Pallas kernels, attend(): pl.pallas_call(functools.partial(attend_kernel, parts), grid=(heads,), in...  21 us
    ppermute x15, starting transfers between devices, across(): return lax.ppermute(value, 'seq', [(i, i ^ bit) for i in range(size)])  18.6 us
    unnamed x78, local copies, waits for them, and re-layouts  18.2 us
    ppermute x15, waiting for transfers between devices, across(): return lax.ppermute(value, 'seq', [(i, i ^ bit) for i in range(size)])  13.2 us
  transfers between devices with their start and end apart: 24, of which 6 were waited for; matrix products, arithmetic and copies ran while one was open for 8% of the time, Pallas kernels for 30%

profile of v1, /device:TPU:0, one launch (start us, length us, event | category | flops | bytes accessed | tf_op | source)
XLA Modules:
  0.0 437.6 jit_solution(16841823446881199785)
XLA Ops:
  0.7 1.3 broadcast_in_dim.47.gain_ref
  2.0 1.3 broadcast_in_dim.46.bias_ref
  3.3 1.3 broadcast_in_dim.48.shift_ref
  5.6 2.0 pad_maximum_fusion.x_ref
  8.4 6.9 %input_linear.1 = (f32[288,1152]{1,0:T(8,128)}, bf16[288,1152]{1,0:T(8,128)(2,1)}, bf16[2304,288]{1,0:T(8,128)(2,1)}) custom-call(bf16[288,1152]{1,0:T(8,128)(2,1)} %pad_maximum_fusion.x_ref, bf16[288,1152]{1,0:T(8,128)(2,1)} %pad_maximum_fusion.1.s_ref, bf16[2304,1152]{1,0:T(8,128)(2,1)} %w_hbm.1, f32[1,1152]{1,0:T(1,128)} %broadcast_in_dim.46.bias_ref, ...), custom_call_target="tpu_custom_call" | custom-call | flops 1528823808 | bytes 9289728 | tf_op jit(solution)/shard_map/input_linear/pallas_call | solution.py:70
  15.4 2.9 collective-permute-start
  20.0 8.1 %heads_weight.1.w_ref.refs_6_ = bf16[4,1152,384]{2,1,0:T(8,128)(2,1)} custom-call(s32[1]{0:T(128)} %bitcast.place_ref, bf16[1152,3456]{1,0:T(8,128)(2,1)} %w_ref.3), custom_call_target="tpu_custom_call" | custom-call | flops 1000000 | bytes 11501568 | tf_op jit(solution)/shard_map/heads_weight/pallas_call | solution.py:106
  29.0 1.0 and_select_fusion.kbias_ref
  30.0 3.4 collective-permute-done
  33.5 1.7 collective-permute-start.2
  37.7 4.8 %collective-permute-done.2 = bf16[144,1152]{1,0:T(8,128)(2,1)S(1)} collective-permute-done((bf16[144,1152]{1,0:T(8,128)(2,1)S(1)}, bf16[144,1152]{1,0:T(8,128)(2,1)S(1)}, u32[]{:S(2)}, u32[]{:S(2)}) %collective-permute-start.2) | collective-permute-done | bytes 331808 | tf_op jit(solution)/shard_map/ppermute | solution.py:610
  44.4 21.0 %attend.1 = (bf16[4,1152,384]{2,1,0:T(8,128)(2,1)}, f32[4,1,1152]{2,1,0:T(1,128)}, bf16[288,288]{1,0:T(8,128)(2,1)}, bf16[288,288]{1,0:T(8,128)(2,1)}, bf16[288,...) custom-call(bf16[1152,1152]{1,0:T(8,128)(2,1)} %constant_dynamic-update-slice_fusion.normed_ref.normed_hbm, ...), custom_call_target="tpu_custom_call" | custom-call | flops 9512681472 | bytes 7962624 | tf_op jit(solution)/shard_map/attend/pallas_call | solution.py:159
  65.5 1.1 collective-permute-start.4
  66.6 1.1 collective-permute-start.5
  67.6 1.4 collective-permute-start.6
  72.0 1.5 collective-permute-done.4.refs_1_
  73.4 3.2 collective-permute-done.5.refs_2_
  77.4 30.1 %feed_forward.1 = (f32[288,1152]{1,0:T(8,128)}, f32[288,1152]{1,0:T(8,128)}, bf16[288,1152]{1,0:T(8,128)(2,1)}, bf16[4608,288]{1,0:T(8,128)(2,1)}, bf16[288,4608...) custom-call(s32[1]{0:T(128)} %bitcast.place_ref, ...), custom_call_target="tpu_custom_call" | custom-call | flops 12230590464 | bytes 29196288 | tf_op jit(solution)/shard_map/feed_forward/pallas_call | solution.py:385
  107.6 1.6 convert_dynamic-update-slice_fusion.3
  111.1 1.5 collective-permute-start.9
  112.6 1.7 constant_dynamic-slice_fusion.7
  114.3 2.4 copy.50
  117.4 1.3 slice_bitcast_fusion.4
  118.8 2.2 copy.52
  126.4 2.3 copy.51.refs_1_
  129.9 1.0 collective-permute-start.17
  130.9 23.3 %pair_grads.1.late_hbm = bf16[4,720,1152]{2,1,0:T(8,128)(2,1)} custom-call(s32[2]{0:T(128)} %pad_add_fusion.where_ref, bf16[4,2,576,288]{3,2,1,0:T(8,128)(2,1)} %bitcast.43, bf16[4,576,288]{2,1,0:T(8,128)(2,1)} %copy.51.refs_1_, bf16[288,1152]{1,0:T(8,128)(2,1)} %copy-done.1, bf16[288,1152]{1,0:T(8,128)(2,1)} %collective-permute-done.11.refs_3_, ...), custom_call_target="tpu_custom_call" | custom-call | flops 3822059520 | bytes 13271040 | tf_op jit(solution)/shard_map/pair_grads/pallas_call | solution.py:496
  154.2 1.6 collective-permute-start.18
  155.8 10.3 %column_grads.1 = bf16[4,4,144,1152]{3,2,1,0:T(8,128)(2,1)} custom-call(s32[2]{0:T(128)} %pad_add_fusion.where_ref, bf16[4,2,144,288]{3,2,1,0:T(8,128)(2,1)} %bitcast.44, bf16[4,144,288]{2,1,0:T(8,128)(2,1)} %copy-done.17, bf16[288,4608]{1,0:T(8,128)(2,1)} %get-tuple-element.78.own, bf16[288,4608]{1,0:T(8,128)(2,1)} %collective-permute-done.15.peer), custom_call_target="tpu_custom_call" | custom-call | flops 3057647616 | bytes 10616832 | tf_op jit(solution)/shard_map/column_grads/pallas_call | solution.py:519
  166.1 4.2 slice_bitcast_fusion
  170.3 4.7 %collective-permute-start.19 = (bf16[720,1152]{1,0:T(8,128)(2,1)}, bf16[720,1152]{1,0:T(8,128)(2,1)}, u32[]{:S(2)}, u32[]{:S(2)}) collective-permute-start(bf16[720,1152]{1,0:T(8,128)(2,1)} %get-tuple-element.175), channel_id=1, source_target_pairs={{0,8},{4,12},{1,9},{5,13},{2,10},{6,14},{3,11},{7,15}} | collective-permute-start | bytes 4976648 | tf_op jit(solution)/shard_map/ppermute | solution.py:1443
  175.0 1.9 collective-permute-start.20
  176.9 2.0 fusion.2
  179.6 1.2 collective-permute-start.22
  180.8 38.9 %attend_back.1 = (bf16[864,1152]{1,0:T(8,128)(2,1)}, bf16[4,144,1152]{2,1,0:T(8,128)(2,1)}, bf16[4,144,1152]{2,1,0:T(8,128)(2,1)}) custom-call(bf16[288,288]{1,0:T(8,128)(2,1)} %get-tuple-element.84.refs_0_, bf16[288,288]{1,0:T(8,128)(2,1)} %copy-done.30, bf16[288,288]{1,0:T(8,128)(2,1)} %copy-done.31, bf16[288,288]{1,0:T(8,128)(2,1)} %copy-done.32, ...), custom_call_target="tpu_custom_call" | custom-call | flops 17666408448 | bytes 15925248 | tf_op jit(solution)/shard_map/attend_back/pallas_call | solution.py:261
  219.7 2.7 add_convert_fusion.first_b_hbm
  222.5 1.4 add_convert_fusion.1.first_a_hbm
  223.8 190.6 %reduce_all.1 = (f32[720,1152]{1,0:T(8,128)}, f32[144,4608]{1,0:T(8,128)}, f32[144,3456]{1,0:T(8,128)}, f32[288,1152]{1,0:T(8,128)}, f32[288,1152]{1,0:T(8,128)}...) custom-call(bf16[4,720,1152]{2,1,0:T(8,128)(2,1)} %pair_grads.1.late_hbm, ...), custom_call_target="tpu_custom_call" | custom-call | flops 10000000000 | bytes 100000000 | tf_op jit(solution)/shard_map/reduce_all/pallas_call | solution.py:1308
  414.5 3.5 slice.99
  418.0 2.1 slice.94
  420.2 2.2 copy.53
  422.5 2.2 copy.55
  424.8 1.1 copy.54
  425.9 1.1 copy.56
  432.1 1.1 copy.69
  433.2 1.3 copy.70
  434.5 1.2 copy-done.2
  435.7 1.5 copy.71
  (147 shorter events, 27.2 us)
Async XLA Ops:
  0.7 6.9 %copy-start.12 = (bf16[256,1,1152]{2,0,1:T(8,128)(2,1)S(1)}, bf16[256,1,1152]{2,0,1:T(8,128)(2,1)}, u32[]{:S(2)}) copy-start(bf16[256,1,1152]{2,0,1:T(8,128)(2,1)} %param.22) | copy-start | bytes 1769476
  8.4 10.5 %copy-start.18 = (bf16[78,1,1152]{2,0,1:T(8,128)(2,1)S(1)}, bf16[78,1,1152]{2,0,1:T(8,128)(2,1)}, u32[]{:S(2)}) copy-start(bf16[78,1,1152]{2,0,1:T(8,128)(2,1)} %param.39) | copy-start | bytes 539140
  8.4 10.5 %copy-start.13 = (bf16[256,1,1152]{2,0,1:T(8,128)(2,1)S(1)}, bf16[256,1,1152]{2,0,1:T(8,128)(2,1)}, u32[]{:S(2)}) copy-start(bf16[256,1,1152]{2,0,1:T(8,128)(2,1)} %param.38) | copy-start | bytes 1769476
  15.4 18.1 %collective-permute-start = (bf16[288,1152]{1,0:T(8,128)(2,1)}, bf16[288,1152]{1,0:T(8,128)(2,1)S(1)}, u32[]{:S(2)}, u32[]{:S(2)}) collective-permute-start(bf16[288,1152]{1,0:T(8,128)(2,1)} %get-tuple-element.67), channel_id=1, source_target_pairs={{0,1},{1,0},{2,3},{3,2},{4,5},{5,4},{6,7},{7,6},{8,9},{9,8},{10,11... | collective-permute-start | bytes 1990664 | tf_op jit(solution)/shard_map/ppermute | solution.py:610
  18.3 16.9 %collective-permute-start.1 = (bf16[288,1152]{1,0:T(8,128)(2,1)}, bf16[288,1152]{1,0:T(8,128)(2,1)S(1)}, u32[]{:S(2)}, u32[]{:S(2)}) collective-permute-start(bf16[288,1152]{1,0:T(8,128)(2,1)} %get-tuple-element.67), channel_id=1, source_target_pairs={{0,2},{1,3},{2,0},{3,1},{4,6},{5,7},{6,4},{7,5},{8,10},{9,11},{10,... | collective-permute-start | bytes 1990664 | tf_op jit(solution)/shard_map/ppermute | solution.py:610
  19.0 9.1 %copy-start.1 = (bf16[288,1152]{1,0:T(8,128)(2,1)}, bf16[288,1152]{1,0:T(8,128)(2,1)S(1)}, u32[]{:S(2)}) copy-start(bf16[288,1152]{1,0:T(8,128)(2,1)S(1)} %pad_maximum_fusion.2.refs_5_.refs_2_) | copy-start | bytes 1990660
  19.0 109.7 %collective-permute-start.11 = (bf16[288,1152]{1,0:T(8,128)(2,1)S(1)}, bf16[288,1152]{1,0:T(8,128)(2,1)}, u32[]{:S(2)}, u32[]{:S(2)}) collective-permute-start(bf16[288,1152]{1,0:T(8,128)(2,1)S(1)} %pad_maximum_fusion.2.refs_5_.refs_2_), channel_id=1, source_target_pairs={{0,4},{4,0},{8,12},{12,8},{16,20},{20,16},{24,28},{28,24},{1,5},{5... | collective-permute-start | bytes 1990664 | tf_op jit(solution)/shard_map/ppermute | solution.py:614
  20.0 8.1 %copy-start.11 = (bf16[288,1152]{1,0:T(8,128)(2,1)S(1)}, bf16[288,1152]{1,0:T(8,128)(2,1)}, u32[]{:S(2)}) copy-start(bf16[288,1152]{1,0:T(8,128)(2,1)} %get-tuple-element.67) | copy-start | bytes 1990660
  33.5 9.1 %collective-permute-start.2 = (bf16[144,1152]{1,0:T(8,128)(2,1)S(1)}, bf16[144,1152]{1,0:T(8,128)(2,1)S(1)}, u32[]{:S(2)}, u32[]{:S(2)}) collective-permute-start(bf16[144,1152]{1,0:T(8,128)(2,1)S(1)} %slice.101), channel_id=1, source_target_pairs={{0,2},{1,3},{2,0},{3,1},{4,6},{5,7},{6,4},{7,5},{8,10},{9,11},{10,... | collective-permute-start | bytes 995336 | tf_op jit(solution)/shard_map/ppermute | solution.py:610
  35.2 8.5 %collective-permute-start.3 = (bf16[144,1152]{1,0:T(8,128)(2,1)S(1)}, bf16[144,1152]{1,0:T(8,128)(2,1)S(1)}, u32[]{:S(2)}, u32[]{:S(2)}) collective-permute-start(bf16[144,1152]{1,0:T(8,128)(2,1)S(1)} %slice.102), channel_id=1, source_target_pairs={{0,1},{1,0},{2,3},{3,2},{4,5},{5,4},{6,7},{7,6},{8,9},{9,8},{10,11... | collective-permute-start | bytes 995336 | tf_op jit(solution)/shard_map/ppermute | solution.py:610
  44.4 25.2 %copy-start.22 = (f32[1152]{0:T(1024)S(1)}, f32[1152]{0:T(1024)}, u32[]{:S(2)}) copy-start(f32[1152]{0:T(1024)} %param.31) | copy-start | bytes 13828
  44.4 25.2 %copy-start.23 = (f32[1152]{0:T(1024)S(1)}, f32[1152]{0:T(1024)}, u32[]{:S(2)}) copy-start(f32[1152]{0:T(1024)} %param.32) | copy-start | bytes 13828
  44.4 25.2 %copy-start.24 = (f32[1152]{0:T(1024)S(1)}, f32[1152]{0:T(1024)}, u32[]{:S(2)}) copy-start(f32[1152]{0:T(1024)} %param.33) | copy-start | bytes 13828
  44.4 25.2 %copy-start.25 = (f32[1152]{0:T(1024)S(1)}, f32[1152]{0:T(1024)}, u32[]{:S(2)}) copy-start(f32[1152]{0:T(1024)} %param.37) | copy-start | bytes 13828
  44.4 25.3 %copy-start.20 = (f32[4608]{0:T(1024)S(1)}, f32[4608]{0:T(1024)}, u32[]{:S(2)}) copy-start(f32[4608]{0:T(1024)} %param.35) | copy-start | bytes 55300
  44.4 26.5 %copy-start.16 = (bf16[2304,288]{1,0:T(8,128)(2,1)S(1)}, bf16[2304,288]{1,0:T(8,128)(2,1)}, u32[]{:S(2)}) copy-start(bf16[2304,288]{1,0:T(8,128)(2,1)} %get-tuple-element.103) | copy-start | bytes 3981316
  65.5 8.0 %collective-permute-start.4 = (bf16[288,288]{1,0:T(8,128)(2,1)}, bf16[288,288]{1,0:T(8,128)(2,1)S(1)}, u32[]{:S(2)}, u32[]{:S(2)}) collective-permute-start(bf16[288,288]{1,0:T(8,128)(2,1)} %get-tuple-element.69), channel_id=1, source_target_pairs={{0,1},{1,0},{2,3},{3,2},{4,5},{5,4},{6,7},{7,6},{8,9},{9,8},{10,11... | collective-permute-start | bytes 497672 | tf_op jit(solution)/shard_map/ppermute | solution.py:610
  66.6 10.0 %collective-permute-start.5 = (bf16[288,288]{1,0:T(8,128)(2,1)}, bf16[288,288]{1,0:T(8,128)(2,1)S(1)}, u32[]{:S(2)}, u32[]{:S(2)}) collective-permute-start(bf16[288,288]{1,0:T(8,128)(2,1)} %get-tuple-element.70), channel_id=1, source_target_pairs={{0,2},{1,3},{2,0},{3,1},{4,6},{5,7},{6,4},{7,5},{8,10},{9,11},{10,... | collective-permute-start | bytes 497672 | tf_op jit(solution)/shard_map/ppermute | solution.py:610
  67.6 9.0 %collective-permute-start.6 = (bf16[288,288]{1,0:T(8,128)(2,1)}, bf16[288,288]{1,0:T(8,128)(2,1)S(1)}, u32[]{:S(2)}, u32[]{:S(2)}) collective-permute-start(bf16[288,288]{1,0:T(8,128)(2,1)} %get-tuple-element.71), channel_id=1, source_target_pairs={{0,3},{1,2},{2,1},{3,0},{4,7},{5,6},{6,5},{7,4},{8,11},{9,10},{10,... | collective-permute-start | bytes 497672 | tf_op jit(solution)/shard_map/ppermute | solution.py:610
  73.4 3.2 copy-start.27
  109.1 13.5 %collective-permute-start.7 = (bf16[32,1152]{1,0:T(8,128)(2,1)}, bf16[32,1152]{1,0:T(8,128)(2,1)}, u32[]{:S(2)}, u32[]{:S(2)}) collective-permute-start(bf16[32,1152]{1,0:T(8,128)(2,1)} %get-tuple-element.173), channel_id=1, source_target_pairs={{0,1},{1,0},{2,3},{3,2},{4,5},{5,4},{6,7},{7,6},{8,9},{9,8},{10,11... | collective-permute-start | bytes 221192 | tf_op jit(solution)/shard_map/ppermute | solution.py:610
  110.1 14.0 %collective-permute-start.8 = (bf16[32,1152]{1,0:T(8,128)(2,1)}, bf16[32,1152]{1,0:T(8,128)(2,1)S(1)}, u32[]{:S(2)}, u32[]{:S(2)}) collective-permute-start(bf16[32,1152]{1,0:T(8,128)(2,1)} %get-tuple-element.173), channel_id=1, source_target_pairs={{0,2},{1,3},{2,0},{3,1},{4,6},{5,7},{6,4},{7,5},{8,10},{9,11},{10,... | collective-permute-start | bytes 221192 | tf_op jit(solution)/shard_map/ppermute | solution.py:610
  111.1 13.1 %collective-permute-start.9 = (bf16[32,1152]{1,0:T(8,128)(2,1)}, bf16[32,1152]{1,0:T(8,128)(2,1)S(1)}, u32[]{:S(2)}, u32[]{:S(2)}) collective-permute-start(bf16[32,1152]{1,0:T(8,128)(2,1)} %get-tuple-element.173), channel_id=1, source_target_pairs={{0,3},{1,2},{2,1},{3,0},{4,7},{5,6},{6,5},{7,4},{8,11},{9,10},{10,... | collective-permute-start | bytes 221192 | tf_op jit(solution)/shard_map/ppermute | solution.py:610
  112.6 43.2 %collective-permute-start.15 = (bf16[288,4608]{1,0:T(8,128)(2,1)}, bf16[288,4608]{1,0:T(8,128)(2,1)}, u32[]{:S(2)}, u32[]{:S(2)}) collective-permute-start(bf16[288,4608]{1,0:T(8,128)(2,1)} %get-tuple-element.78.own), channel_id=1, source_target_pairs={{0,4},{4,0},{8,12},{12,8},{16,20},{20,16},{24,28},{28,24},{1,5},{5... | collective-permute-start | bytes 7962632 | tf_op jit(solution)/shard_map/ppermute | solution.py:614
  118.7 3.1 copy-start.5
  118.7 3.9 copy-start.6
  118.8 5.3 %copy-start.10 = (bf16[288,1152]{1,0:T(8,128)(2,1)S(1)}, bf16[288,1152]{1,0:T(8,128)(2,1)}, u32[]{:S(2)}) copy-start(bf16[288,1152]{1,0:T(8,128)(2,1)} %get-tuple-element.76.refs_6_) | copy-start | bytes 1990660
  122.7 3.4 collective-permute-start.10
  124.1 5.8 %collective-permute-start.13 = (bf16[288,1152]{1,0:T(8,128)(2,1)S(1)}, bf16[288,1152]{1,0:T(8,128)(2,1)}, u32[]{:S(2)}, u32[]{:S(2)}) collective-permute-start(bf16[288,1152]{1,0:T(8,128)(2,1)S(1)} %copy-done.10), channel_id=1, source_target_pairs={{0,4},{4,0},{8,12},{12,8},{16,20},{20,16},{24,28},{28,24},{1,5},{5... | collective-permute-start | bytes 1990664 | tf_op jit(solution)/shard_map/ppermute | solution.py:614
  124.2 4.7 %collective-permute-start.12 = (bf16[4,144,288]{2,1,0:T(8,128)(2,1)}, bf16[4,144,288]{2,1,0:T(8,128)(2,1)}, u32[]{:S(2)}, u32[]{:S(2)}) collective-permute-start(bf16[4,144,288]{2,1,0:T(8,128)(2,1)} %dynamic-slice_bitcast_fusion.2), channel_id=1, source_target_pairs={{0,4},{4,0},{8,12},{12,8},{16,20},{20,16},{24,28},{28,24},{1,5},{5... | collective-permute-start | bytes 995336 | tf_op jit(solution)/shard_map/ppermute | solution.py:614
  125.8 3.0 copy-start.15
  126.1 97.8 %collective-permute-start.23 = (bf16[4,288,288]{2,1,0:T(8,128)(2,1)}, bf16[4,288,288]{2,1,0:T(8,128)(2,1)}, u32[]{:S(2)}, u32[]{:S(2)}) collective-permute-start(bf16[4,288,288]{2,1,0:T(8,128)(2,1)} %dynamic-slice_bitcast_fusion), channel_id=1, source_target_pairs={{0,4},{4,0},{8,12},{12,8},{16,20},{20,16},{24,28},{28,24},{1,5},{5... | collective-permute-start | bytes 1990664 | tf_op jit(solution)/shard_map/ppermute | solution.py:614
  128.7 25.4 %collective-permute-start.14 = (bf16[4,144,288]{2,1,0:T(8,128)(2,1)S(1)}, bf16[4,144,288]{2,1,0:T(8,128)(2,1)S(1)}, u32[]{:S(2)}, u32[]{:S(2)}) collective-permute-start(bf16[4,144,288]{2,1,0:T(8,128)(2,1)S(1)} %copy-done.15), channel_id=1, source_target_pairs={{0,4},{4,0},{8,12},{12,8},{16,20},{20,16},{24,28},{28,24},{1,5},{5... | collective-permute-start | bytes 995336 | tf_op jit(solution)/shard_map/ppermute | solution.py:614
  128.9 37.2 %collective-permute-start.16 = (bf16[288,288]{1,0:T(8,128)(2,1)}, bf16[288,288]{1,0:T(8,128)(2,1)S(1)}, u32[]{:S(2)}, u32[]{:S(2)}) collective-permute-start(bf16[288,288]{1,0:T(8,128)(2,1)} %get-tuple-element.80), channel_id=1, source_target_pairs={{0,1},{1,0},{2,3},{3,2},{4,5},{5,4},{6,7},{7,6},{8,9},{9,8},{10,11... | collective-permute-start | bytes 497672 | tf_op jit(solution)/shard_map/ppermute | solution.py:610
  129.8 24.3 %copy-start.26 = (bf16[288,288]{1,0:T(8,128)(2,1)S(1)}, bf16[288,288]{1,0:T(8,128)(2,1)}, u32[]{:S(2)}) copy-start(bf16[288,288]{1,0:T(8,128)(2,1)} %get-tuple-element.82) | copy-start | bytes 497668
  129.9 36.2 %collective-permute-start.17 = (bf16[288,288]{1,0:T(8,128)(2,1)}, bf16[288,288]{1,0:T(8,128)(2,1)S(1)}, u32[]{:S(2)}, u32[]{:S(2)}) collective-permute-start(bf16[288,288]{1,0:T(8,128)(2,1)} %get-tuple-element.81), channel_id=1, source_target_pairs={{0,2},{1,3},{2,0},{3,1},{4,6},{5,7},{6,4},{7,5},{8,10},{9,11},{10,... | collective-permute-start | bytes 497672 | tf_op jit(solution)/shard_map/ppermute | solution.py:610
  154.2 11.9 %collective-permute-start.18 = (bf16[288,288]{1,0:T(8,128)(2,1)S(1)}, bf16[288,288]{1,0:T(8,128)(2,1)S(1)}, u32[]{:S(2)}, u32[]{:S(2)}) collective-permute-start(bf16[288,288]{1,0:T(8,128)(2,1)S(1)} %copy-done.26), channel_id=1, source_target_pairs={{0,3},{1,2},{2,1},{3,0},{4,7},{5,6},{6,5},{7,4},{8,11},{9,10},{10,... | collective-permute-start | bytes 497672 | tf_op jit(solution)/shard_map/ppermute | solution.py:610
  166.1 4.2 copy-start.30
  166.1 4.2 copy-start.31
  166.1 4.2 copy-start.32
  166.1 10.7 %copy-start = (bf16[4,4,144,1152]{3,2,1,0:T(8,128)(2,1)S(1)}, bf16[4,4,144,1152]{3,2,1,0:T(8,128)(2,1)}, u32[]{:S(2)}) copy-start(bf16[4,4,144,1152]{3,2,1,0:T(8,128)(2,1)} %column_grads.1) | copy-start | bytes 15925252
  170.3 49.4 %collective-permute-start.19 = (bf16[720,1152]{1,0:T(8,128)(2,1)}, bf16[720,1152]{1,0:T(8,128)(2,1)}, u32[]{:S(2)}, u32[]{:S(2)}) collective-permute-start(bf16[720,1152]{1,0:T(8,128)(2,1)} %get-tuple-element.175), channel_id=1, source_target_pairs={{0,8},{4,12},{1,9},{5,13},{2,10},{6,14},{3,11},{7,15}} | collective-permute-start | bytes 4976648 | tf_op jit(solution)/shard_map/ppermute | solution.py:1443
  175.0 44.7 %collective-permute-start.20 = (bf16[720,1152]{1,0:T(8,128)(2,1)}, bf16[720,1152]{1,0:T(8,128)(2,1)}, u32[]{:S(2)}, u32[]{:S(2)}) collective-permute-start(bf16[720,1152]{1,0:T(8,128)(2,1)} %get-tuple-element.174), channel_id=1, source_target_pairs={{24,16},{28,20},{25,17},{29,21},{26,18},{30,22},{27,19},{31,23}} | collective-permute-start | bytes 4976648 | tf_op jit(solution)/shard_map/ppermute | solution.py:1444
  178.8 40.9 %collective-permute-start.21 = (bf16[2,2,144,1152]{3,2,1,0:T(8,128)(2,1)}, bf16[2,2,144,1152]{3,2,1,0:T(8,128)(2,1)S(1)}, u32[]{:S(2)}, u32[]{:S(2)}) collective-permute-start(bf16[2,2,144,1152]{3,2,1,0:T(8,128)(2,1)} %get-tuple-element.178), channel_id=1, source_target_pairs={{0,1},{1,0},{2,3},{3,2},{4,5},{5,4},{6,7},{7,6},{8,9},{9,8},{10,11... | collective-permute-start | bytes 3981320 | tf_op jit(solution)/shard_map/ppermute | solution.py:610
  179.6 40.1 %collective-permute-start.22 = (bf16[2,2,144,1152]{3,2,1,0:T(8,128)(2,1)}, bf16[2,2,144,1152]{3,2,1,0:T(8,128)(2,1)}, u32[]{:S(2)}, u32[]{:S(2)}) collective-permute-start(bf16[2,2,144,1152]{3,2,1,0:T(8,128)(2,1)} %get-tuple-element.176), channel_id=1, source_target_pairs={{0,2},{1,3},{2,0},{3,1},{4,6},{5,7},{6,4},{7,5},{8,10},{9,11},{10,... | collective-permute-start | bytes 3981320 | tf_op jit(solution)/shard_map/ppermute | solution.py:610
  414.5 5.5 %copy-start.19 = (f32[16,1152]{1,0:T(8,128)S(1)}, f32[16,1152]{1,0:T(8,128)}, u32[]{:S(2)}) copy-start(f32[16,1152]{1,0:T(8,128)} %get-tuple-element.111) | copy-start | bytes 221188
  424.7 7.4 %copy-start.7 = (f32[288,1152]{1,0:T(8,128)S(1)}, f32[288,1152]{1,0:T(8,128)}, u32[]{:S(2)}) copy-start(f32[288,1152]{1,0:T(8,128)} %get-tuple-element.216) | copy-start | bytes 3981316
  425.9 7.3 %copy-start.4 = (f32[144,3456]{1,0:T(8,128)S(1)}, f32[144,3456]{1,0:T(8,128)}, u32[]{:S(2)}) copy-start(f32[144,3456]{1,0:T(8,128)} %get-tuple-element.220) | copy-start | bytes 5971972
  (9 other events, 16.8 us)
